TPU v7x, 512 devices: a whole 4x8x8 slice. The times are simulated.
512 devices in a mesh: tile: 32 (over y_hi, z, core), layer: 16 (over x, y_lo).
Axes of the slice: x: 4, y: 8 (y_hi: 2, y_lo: 4; y = y_hi * 4 + y_lo), z: 8, core: 2. Of those that a mesh axis runs over, the one named last changes fastest.
Arguments:
- pressure: float32 [64, 256, 2048], P('layer', 'tile'), may hold values from -4 to -0.5
- old_pressure: float32 [64, 256, 2048], P('layer', 'tile'), may hold values from -4 to -0.5
- texture: int32 [64, 256, 2048], P('layer', 'tile'), may hold values from 0 to 11
- zones: int32 [256, 2048], P('tile'), may hold values from 0 to 15
- rates: float32 [16], replicated, may hold values from 0.05 to 0.5
- vg_table: float32 [5, 12], replicated, may hold values from 0.03 to 3, as said below
- approx_inverse: float32 [64, 64], replicated, may hold values from -0.2 to 0.36, as said below
Outputs:
- new_pressure: float32 [64, 256, 2048], P('layer', 'tile')
Inputs may be any that keep to these rules, and one draw needn't show every extreme that they name: `vg_table`: rows are inverse scale in 0.5 to 3, n in 1.3 to 2.7, residual content in 0.03 to 0.1, saturated content in 0.35 to 0.5, saturated conductivity in 0.05 to 0.5. `approx_inverse`: diagonal in 0.24 to 0.36, off-diagonal entries of deviation 0.02.
All inputs are finite; a program needn't handle non-finite values.
Results may differ from a plain program's by a relative error of at most 0.0001.
Values sent between devices are 32-bit elements; how exact they have to be, the bound alone decides.
A program may use at most 64 MiB of HBM per device.

v0:
```python
import jax
import jax.numpy as jnp
from jax import lax
from jax.sharding import PartitionSpec as P

ITERS = 3
SWEEPS = 2


DT = 1.0
DZ = 1.0
OMEGA = 0.2


def with_halo(block, sides, width):
    for axis, dim in sides:
        count = lax.axis_size(axis)
        forward = [(i, i + 1) for i in range(count - 1)]
        backward = [(target, source) for source, target in forward]
        low = lax.ppermute(
            lax.slice_in_dim(block, block.shape[dim] - width, None, axis=dim), axis, forward
        )
        high = lax.ppermute(lax.slice_in_dim(block, 0, width, axis=dim), axis, backward)
        block = jnp.concatenate([low, block, high], axis=dim)
    return block


def closures(pressure, params):
    inv_scale, exponent, residual_wc, saturated_wc, saturated_k = params
    suction = jax.nn.softplus(-pressure)
    power = 1.0 - 1.0 / exponent
    saturation = (1.0 + (inv_scale * suction) ** exponent) ** (-power)
    moisture = residual_wc + (saturated_wc - residual_wc) * saturation
    conduct = saturated_k * saturation * saturation * saturation
    return (moisture, conduct)


def lookup(texture, vg_table):
    fields = []
    for row in range(5):
        total = jnp.zeros(texture.shape, jnp.float32)
        for klass in range(vg_table.shape[1]):
            total = total + jnp.where(texture == klass, vg_table[row, klass], 0.0)
        fields.append(total)
    return tuple(fields)


def zone_rate(zone_ids, rates):
    ladder = jnp.arange(rates.shape[0], dtype=jnp.int32)
    return jnp.sum(jnp.where(zone_ids[..., None] == ladder, rates, 0.0), axis=-1)


def lateral(pressure, params, weight):
    moisture, conduct = closures(pressure, params)
    extended = with_halo(jnp.stack([pressure, conduct]), (("tile", 2),), 1)
    head_ext = extended[0]
    cond_ext = extended[1]
    flow_x = 0.5 * (cond_ext[:, 1:] + cond_ext[:, :-1]) * (head_ext[:, 1:] - head_ext[:, :-1])
    flow_x = flow_x * weight[None, :, None]
    change = flow_x[:, 1:] - flow_x[:, :-1]
    flow_y = (
        0.5 * (conduct[:, :, 1:] + conduct[:, :, :-1]) * (pressure[:, :, 1:] - pressure[:, :, :-1])
    )
    change = change + (
        jnp.pad(flow_y, ((0, 0), (0, 0), (0, 1))) - jnp.pad(flow_y, ((0, 0), (0, 0), (1, 0)))
    )
    return pressure + OMEGA * change


def body(pressure, old_pressure, texture, zones, rates, vg_table, approx_inverse):
    params = lookup(texture, vg_table)
    group_rows = pressure.shape[0]
    layer_index = lax.axis_index("layer")
    layer_count = lax.axis_size("layer")
    moisture_old, unused = closures(old_pressure, params)
    inflow = zone_rate(zones, rates)
    own_first = layer_index * group_rows
    for newton_index in range(ITERS):
        moisture, conduct = closures(pressure, params)
        extended = with_halo(jnp.stack([pressure, conduct]), (("layer", 1),), 1)
        head_ext = extended[0]
        cond_ext = extended[1]
        interface = 0.5 * (cond_ext[:-1] + cond_ext[1:])
        fluxes = interface * ((head_ext[:-1] - head_ext[1:]) / DZ + 1.0)
        top_flux = jnp.where(layer_index == 0, inflow[None], fluxes[:1])
        bottom_flux = jnp.where(layer_index == layer_count - 1, conduct[-1:], fluxes[-1:])
        fluxes = jnp.concatenate([top_flux, fluxes[1:-1], bottom_flux], axis=0)
        misfit = (moisture - moisture_old) / DT + (fluxes[1:] - fluxes[:-1]) / DZ
        piece = lax.all_gather(misfit, "layer", axis=0, tiled=True)
        block = lax.dynamic_slice(approx_inverse, (own_first, 0), (group_rows, piece.shape[0]))
        product = jnp.dot(block, piece.reshape(piece.shape[0], -1), precision=lax.Precision.HIGHEST)
        update = product.reshape(jnp.zeros(misfit.shape, jnp.float32).shape)
        pressure = pressure - update
    tile_index = lax.axis_index("tile")
    tile_count = lax.axis_size("tile")
    left_open = (tile_index > 0).astype(jnp.float32)
    right_open = (tile_index < tile_count - 1).astype(jnp.float32)
    weight = jnp.concatenate(
        [left_open[None], jnp.ones((pressure.shape[1] - 1,), jnp.float32), right_open[None]]
    )
    for sweep_index in range(SWEEPS):
        pressure = lateral(pressure, params, weight)
    return pressure


def solution(mesh):
    placed = (
        P("layer", "tile", None),
        P("layer", "tile", None),
        P("layer", "tile", None),
        P("tile", None),
        P(),
        P(),
        P(),
    )
    return jax.shard_map(
        body, mesh=mesh, in_specs=placed, out_specs=P("layer", "tile", None), check_vma=False
    )
```

profile of v0, /device:TPU:56, one launch (start us, length us, event | category | flops | bytes accessed | tf_op | source)
XLA Modules:
  0.0 484.3 jit_solution(6300479955119043251)
XLA Ops:
  6.5 1.4 fusion.86
  8.0 2.1 fusion.84
  10.1 2.1 fusion.83
  12.2 1.1 copy.204
  13.3 27.9 %multiply_multiply_fusion.4 = (f32[4,8,2048]{2,0,1:T(4,128)S(1)}, f32[4,8,2048]{2,0,1:T(4,128)S(1)}, f32[4,8,2048]{2,0,1:T(4,128)S(1)}, f32[4,8,2048]{2,0,1:T(4,...) fusion(f32[]{:T(128)} %bitcast.61, f32[]{:T(128)} %bitcast.60, ...), kind=kLoop, calls=%fused_computation.45 | loop fusion | flops 6291456 | bytes 2621584 | tf_op jit(solution)/shard_map/mul | solution.py:34
  41.5 5.8 %collective-permute-start = (f32[2,1,8,2048]{3,1,2,0:T(1,128)S(1)}, f32[2,1,8,2048]{3,1,2,0:T(1,128)S(1)}, u32[]{:S(2)}, u32[]{:S(2)}) collective-permute-start(f32[2,1,8,2048]{3,1,2,0:T(1,128)S(1)} %get-tuple-element.55), channel_id=1, source_target_pairs={{0,1},{1,2},{2,3},{3,4},{4,5},{5,6},{6,7},{7,8},{8,9},{9,10},{10,1... | collective-permute-start | bytes 393224 | tf_op jit(solution)/shard_map/ppermute | solution.py:20
  47.3 1.9 collective-permute-start.1
  49.2 2.1 fusion.85
  52.3 4.5 collective-permute-done.1
  57.6 18.5 %fusion.67 = (f32[4,8,2048]{2,0,1:T(4,128)S(1)}, f32[4,8,2048]{2,0,1:T(4,128)S(1)}, f32[4,8,2048]{2,0,1:T(4,128)S(1)}) fusion(f32[1,8,2048]{2,0,1:T(1,128)S(1)} %get-tuple-element.52, f32[3,8,2048]{2,0,1:T(4,128)S(1)} %slice_bitcast_fusion.4, f32[1,8,2048]{2,0,1:T(1,128)S(1)} %get-tuple-element.51, f32[4,8,2048]{2,0,1:T(4,128)S(1)} %get-tuple-element.16, ...), kind=kLoop, calls=%fused_computation.106 | loop fusion | flops 4456448 | bytes 2949216 | tf_op jit(solution)/shard_map/add | solution.py:88
  77.6 104.6 %all-gather.4.cloned.1.call-done = f32[64,8,2048]{2,1,0:T(8,128)} async-done(((f32[4,8,2048]{2,1,0:T(8,128)}), f32[64,8,2048]{2,1,0:T(8,128)}) %all-gather.4.cloned.1.call-update) | async-done | bytes 4194320 | tf_op jit(solution)/shard_map/all_gather | solution.py:89
  182.2 8.2 %multiply_multiply_fusion.3 = (f32[4,8,2048]{2,0,1:T(4,128)S(1)}, f32[4,8,2048]{2,0,1:T(4,128)S(1)}, f32[4,8,2048]{2,0,1:T(4,128)S(1)}) fusion(f32[4,8,2048]{2,0,1:T(4,128)S(1)} %get-tuple-element.15, f32[4,8,2048]{2,0,1:T(4,128)S(1)} %get-tuple-element.18, f32[4,8,2048]{2,0,1:T(4,128)S(1)} %get-tuple-element.17, f32[64,64]{1,0:T(8,128)S(1)} %copy-done, ...), kind=kOutput, calls=%fused_computation.44 | convolution fusion | flops 51380224 | bytes 6031364 | tf_op jit(solution)/shard_map/dot_general | solution.py:91
  190.6 2.8 collective-permute-start.2
  193.4 3.0 collective-permute-start.3
  196.4 1.3 collective-permute-done.2
  197.7 5.2 %collective-permute-done.3 = f32[2,1,8,2048]{3,1,2,0:T(1,128)S(1)} collective-permute-done((f32[2,1,8,2048]{3,1,2,0:T(1,128)S(1)}, f32[2,1,8,2048]{3,1,2,0:T(1,128)S(1)}, u32[]{:S(2)}, u32[]{:S(2)}) %collective-permute-start.3) | collective-permute-done | bytes 131104 | tf_op jit(solution)/shard_map/ppermute | solution.py:23
  204.4 2.6 fusion.68
  208.1 102.0 %all-gather.6.cloned.1.call-done = f32[64,8,2048]{2,1,0:T(8,128)} async-done(((f32[4,8,2048]{2,1,0:T(8,128)}), f32[64,8,2048]{2,1,0:T(8,128)}) %all-gather.6.cloned.1.call-update) | async-done | bytes 4194320 | tf_op jit(solution)/shard_map/all_gather | solution.py:89
  310.1 8.2 %multiply_multiply_fusion.2 = (f32[4,8,2048]{2,0,1:T(4,128)S(1)}, f32[4,8,2048]{2,0,1:T(4,128)S(1)}, f32[4,8,2048]{2,0,1:T(4,128)S(1)}) fusion(f32[4,8,2048]{2,0,1:T(4,128)S(1)} %get-tuple-element.15, f32[4,8,2048]{2,0,1:T(4,128)S(1)} %get-tuple-element.18, f32[4,8,2048]{2,0,1:T(4,128)S(1)} %get-tuple-element.17, f32[4,8,2048]{2,0,1:T(4,128)S(1)} %get-tuple-element.121, ...), kind=kOutput, calls=%fused_computation.43 | convolution fusion | flops 51380224 | bytes 6031364 | tf_op jit(solution)/shard_map/dot_general | solution.py:91
  318.5 2.8 collective-permute-start.4
  321.3 3.2 collective-permute-start.5
  325.6 5.2 %collective-permute-done.5 = f32[2,1,8,2048]{3,1,2,0:T(1,128)S(1)} collective-permute-done((f32[2,1,8,2048]{3,1,2,0:T(1,128)S(1)}, f32[2,1,8,2048]{3,1,2,0:T(1,128)S(1)}, u32[]{:S(2)}, u32[]{:S(2)}) %collective-permute-start.5) | collective-permute-done | bytes 131104 | tf_op jit(solution)/shard_map/ppermute | solution.py:23
  332.3 2.6 fusion.69
  335.8 102.1 %all-gather.8.cloned.1.call-done = f32[64,8,2048]{2,1,0:T(8,128)} async-done(((f32[4,8,2048]{2,1,0:T(8,128)}), f32[64,8,2048]{2,1,0:T(8,128)}) %all-gather.8.cloned.1.call-update) | async-done | bytes 4194320 | tf_op jit(solution)/shard_map/all_gather | solution.py:89
  438.0 8.2 %multiply_multiply_fusion.1 = (f32[4,8,2048]{2,0,1:T(4,128)S(1)}, f32[4,8,2048]{2,0,1:T(4,128)S(1)}) fusion(f32[4,8,2048]{2,0,1:T(4,128)S(1)} %get-tuple-element.15, f32[4,8,2048]{2,0,1:T(4,128)S(1)} %get-tuple-element.18, f32[4,8,2048]{2,0,1:T(4,128)S(1)} %get-tuple-element.17, f32[4,8,2048]{2,0,1:T(4,128)S(1)} %get-tuple-element.122, ...), kind=kOutput, calls=%fused_computation.42 | convolution fusion | flops 51380224 | bytes 5769220 | tf_op jit(solution)/shard_map/dot_general | solution.py:91
  446.2 1.9 collective-permute-start.6
  448.1 9.9 %collective-permute-start.7 = (f32[2,4,1,2048]{3,1,2,0:T(4,128)S(1)}, f32[2,4,1,2048]{3,1,2,0:T(4,128)S(1)}, u32[]{:S(2)}, u32[]{:S(2)}) collective-permute-start(f32[2,4,1,2048]{3,1,2,0:T(4,128)S(1)} %get-tuple-element.42), channel_id=1, source_target_pairs={{16,0},{32,16},{48,32},{64,48},{80,64},{96,80},{112,96},{128,112},... | collective-permute-start | bytes 196616 | tf_op jit(solution)/shard_map/ppermute | solution.py:23
  458.4 1.3 collective-permute-done.7
  460.1 2.3 multiply_multiply_fusion
  462.4 1.9 collective-permute-start.8
  464.4 9.7 %collective-permute-start.9 = (f32[2,4,1,2048]{3,1,2,0:T(4,128)S(1)}, f32[2,4,1,2048]{3,1,2,0:T(4,128)S(1)}, u32[]{:S(2)}, u32[]{:S(2)}) collective-permute-start(f32[2,4,1,2048]{3,1,2,0:T(4,128)S(1)} %get-tuple-element.40), channel_id=1, source_target_pairs={{16,0},{32,16},{48,32},{64,48},{80,64},{96,80},{112,96},{128,112},... | collective-permute-start | bytes 196616 | tf_op jit(solution)/shard_map/ppermute | solution.py:23
  474.5 1.5 collective-permute-done.9
  (55 shorter events, 12.3 us)
Async XLA Ops:
  6.5 175.6 %copy-start = (f32[64,64]{1,0:T(8,128)S(1)}, f32[64,64]{1,0:T(8,128)}, u32[]{:S(2)}) copy-start(f32[64,64]{1,0:T(8,128)} %param.13) | copy-start | bytes 49156
  6.5 44.8 %copy-start.3 = (s32[8,2048]{1,0:T(8,128)S(1)}, s32[8,2048]{1,0:T(8,128)}, u32[]{:S(2)}) copy-start(s32[8,2048]{1,0:T(8,128)} %param.10) | copy-start | bytes 196612
  6.5 175.6 %all-gather.4.cloned.1.call-start = ((), (), s32[]{:S(2)}) async-start(), calls=%async_computation | async-start | bytes 4456448 | tf_op jit(solution)/shard_map/all_gather | solution.py:89
  41.3 16.4 %copy-start.1 = (f32[4,8,2048]{2,1,0:T(8,128)S(1)}, f32[4,8,2048]{2,1,0:T(8,128)}, u32[]{:S(2)}) copy-start(f32[4,8,2048]{2,1,0:T(8,128)} %param.8) | copy-start | bytes 786436
  41.5 10.8 %collective-permute-start = (f32[2,1,8,2048]{3,1,2,0:T(1,128)S(1)}, f32[2,1,8,2048]{3,1,2,0:T(1,128)S(1)}, u32[]{:S(2)}, u32[]{:S(2)}) collective-permute-start(f32[2,1,8,2048]{3,1,2,0:T(1,128)S(1)} %get-tuple-element.55), channel_id=1, source_target_pairs={{0,1},{1,2},{2,3},{3,4},{4,5},{5,6},{6,7},{7,8},{8,9},{9,10},{10,1... | collective-permute-start | bytes 393224 | tf_op jit(solution)/shard_map/ppermute | solution.py:20
  47.3 9.6 %collective-permute-start.1 = (f32[2,1,8,2048]{3,1,2,0:T(1,128)S(1)}, f32[2,1,8,2048]{3,1,2,0:T(1,128)S(1)}, u32[]{:S(2)}, u32[]{:S(2)}) collective-permute-start(f32[2,1,8,2048]{3,1,2,0:T(1,128)S(1)} %get-tuple-element.56), channel_id=1, source_target_pairs={{1,0},{2,1},{3,2},{4,3},{5,4},{6,5},{7,6},{8,7},{9,8},{10,9},{11,1... | collective-permute-start | bytes 393224 | tf_op jit(solution)/shard_map/ppermute | solution.py:23
  57.2 124.9 %copy-start.2 = (f32[4,8,2048]{2,1,0:T(8,128)S(1)}, f32[4,8,2048]{2,1,0:T(8,128)}, u32[]{:S(2)}) copy-start(f32[4,8,2048]{2,1,0:T(8,128)} %param.7) | copy-start | bytes 786436
  77.0 233.1 %all-gather.6.cloned.1.call-start = ((), (), s32[]{:S(2)}) async-start(), calls=%async_computation.1 | async-start | bytes 4456448 | tf_op jit(solution)/shard_map/all_gather | solution.py:89
  190.6 7.1 %collective-permute-start.2 = (f32[2,1,8,2048]{3,1,2,0:T(1,128)S(1)}, f32[2,1,8,2048]{3,1,2,0:T(1,128)S(1)}, u32[]{:S(2)}, u32[]{:S(2)}) collective-permute-start(f32[2,1,8,2048]{3,1,2,0:T(1,128)S(1)} %get-tuple-element.49), channel_id=1, source_target_pairs={{0,1},{1,2},{2,3},{3,4},{4,5},{5,6},{6,7},{7,8},{8,9},{9,10},{10,1... | collective-permute-start | bytes 393224 | tf_op jit(solution)/shard_map/ppermute | solution.py:20
  193.4 9.6 %collective-permute-start.3 = (f32[2,1,8,2048]{3,1,2,0:T(1,128)S(1)}, f32[2,1,8,2048]{3,1,2,0:T(1,128)S(1)}, u32[]{:S(2)}, u32[]{:S(2)}) collective-permute-start(f32[2,1,8,2048]{3,1,2,0:T(1,128)S(1)} %get-tuple-element.50), channel_id=1, source_target_pairs={{1,0},{2,1},{3,2},{4,3},{5,4},{6,5},{7,6},{8,7},{9,8},{10,9},{11,1... | collective-permute-start | bytes 393224 | tf_op jit(solution)/shard_map/ppermute | solution.py:23
  207.8 230.1 %all-gather.8.cloned.1.call-start = ((), (), s32[]{:S(2)}) async-start(), calls=%async_computation.2 | async-start | bytes 4456448 | tf_op jit(solution)/shard_map/all_gather | solution.py:89
  318.5 7.1 %collective-permute-start.4 = (f32[2,1,8,2048]{3,1,2,0:T(1,128)S(1)}, f32[2,1,8,2048]{3,1,2,0:T(1,128)S(1)}, u32[]{:S(2)}, u32[]{:S(2)}) collective-permute-start(f32[2,1,8,2048]{3,1,2,0:T(1,128)S(1)} %get-tuple-element.45), channel_id=1, source_target_pairs={{0,1},{1,2},{2,3},{3,4},{4,5},{5,6},{6,7},{7,8},{8,9},{9,10},{10,1... | collective-permute-start | bytes 393224 | tf_op jit(solution)/shard_map/ppermute | solution.py:20
  321.3 9.6 %collective-permute-start.5 = (f32[2,1,8,2048]{3,1,2,0:T(1,128)S(1)}, f32[2,1,8,2048]{3,1,2,0:T(1,128)S(1)}, u32[]{:S(2)}, u32[]{:S(2)}) collective-permute-start(f32[2,1,8,2048]{3,1,2,0:T(1,128)S(1)} %get-tuple-element.46), channel_id=1, source_target_pairs={{1,0},{2,1},{3,2},{4,3},{5,4},{6,5},{7,6},{8,7},{9,8},{10,9},{11,1... | collective-permute-start | bytes 393224 | tf_op jit(solution)/shard_map/ppermute | solution.py:23
  446.2 12.2 %collective-permute-start.6 = (f32[2,4,1,2048]{3,1,2,0:T(4,128)S(1)}, f32[2,4,1,2048]{3,1,2,0:T(4,128)S(1)}, u32[]{:S(2)}, u32[]{:S(2)}) collective-permute-start(f32[2,4,1,2048]{3,1,2,0:T(4,128)S(1)} %get-tuple-element.41), channel_id=1, source_target_pairs={{0,16},{16,32},{32,48},{48,64},{64,80},{80,96},{96,112},{112,128},... | collective-permute-start | bytes 196616 | tf_op jit(solution)/shard_map/ppermute | solution.py:20
  448.1 11.6 %collective-permute-start.7 = (f32[2,4,1,2048]{3,1,2,0:T(4,128)S(1)}, f32[2,4,1,2048]{3,1,2,0:T(4,128)S(1)}, u32[]{:S(2)}, u32[]{:S(2)}) collective-permute-start(f32[2,4,1,2048]{3,1,2,0:T(4,128)S(1)} %get-tuple-element.42), channel_id=1, source_target_pairs={{16,0},{32,16},{48,32},{64,48},{80,64},{96,80},{112,96},{128,112},... | collective-permute-start | bytes 196616 | tf_op jit(solution)/shard_map/ppermute | solution.py:23
  462.4 12.0 %collective-permute-start.8 = (f32[2,4,1,2048]{3,1,2,0:T(4,128)S(1)}, f32[2,4,1,2048]{3,1,2,0:T(4,128)S(1)}, u32[]{:S(2)}, u32[]{:S(2)}) collective-permute-start(f32[2,4,1,2048]{3,1,2,0:T(4,128)S(1)} %get-tuple-element.39), channel_id=1, source_target_pairs={{0,16},{16,32},{32,48},{48,64},{64,80},{80,96},{96,112},{112,128},... | collective-permute-start | bytes 196616 | tf_op jit(solution)/shard_map/ppermute | solution.py:20
  464.4 11.6 %collective-permute-start.9 = (f32[2,4,1,2048]{3,1,2,0:T(4,128)S(1)}, f32[2,4,1,2048]{3,1,2,0:T(4,128)S(1)}, u32[]{:S(2)}, u32[]{:S(2)}) collective-permute-start(f32[2,4,1,2048]{3,1,2,0:T(4,128)S(1)} %get-tuple-element.40), channel_id=1, source_target_pairs={{16,0},{32,16},{48,32},{64,48},{80,64},{96,80},{112,96},{128,112},... | collective-permute-start | bytes 196616 | tf_op jit(solution)/shard_map/ppermute | solution.py:23
Sparse Core Ops, SparseCore 0:
  77.1 104.9 all-gather.3
  208.0 102.0 all-gather.5
  335.9 102.0 all-gather.7
where the time goes:
time: 492 us; the launch traced here: 484 us
  waiting for transfers between devices  329 us (67%)
  other arithmetic  60.3 us (12%)
  starting transfers between devices  43.8 us (9%)
  matrix products  24.5 us (5%)
  between operations  13.8 us (3%)
  local copies, waits for them, and re-layouts  12.8 us (3%)
    all_gather x3, waiting for transfers between devices, body(): piece = lax.all_gather(misfit, 'layer', axis=0, tiled=True)  309 us
    mul x2, other arithmetic, closures(): conduct = saturated_k * saturation * saturation * saturation  30.3 us
    ppermute x5, starting transfers between devices, with_halo(): lax.ppermute(lax.slice_in_dim(block, 0, width, axis=dim), axis, backward)  27.8 us
    dot_general x3, matrix products, body(): jnp.dot(block, piece.reshape(piece.shape[0], -1), precision=lax.Precision...  24.5 us
    add x3, other arithmetic, body(): misfit = (moisture - moisture_old) / DT + (fluxes[1:] - fluxes[:-1]) / DZ  23.6 us
    ppermute x5, waiting for transfers between devices, with_halo(): lax.ppermute(lax.slice_in_dim(block, 0, width, axis=dim), axis, backward)  17.8 us
    ppermute x5, starting transfers between devices, with_halo(): lax.ppermute(lax.slice_in_dim(block, block.shape[dim] - width, None, axis...  15.2 us
  transfers between devices with their start and end apart: 13, of which 10 were waited for; matrix products, arithmetic and copies ran while one was open for 1% of the time, Pallas kernels for 0%

commit v1 on v0

v1 whole, which is shorter than its diff:
```python
import functools

import jax
import jax.numpy as jnp
from jax import lax
from jax.experimental import pallas as pl
from jax.experimental.pallas import tpu as pltpu
from jax.sharding import PartitionSpec as P

ITERS = 3
SWEEPS = 2
OMEGA = 0.2
LOG2E = 1.4426950408889634
MESH = pl.DeviceIdType.MESH
LANES = 128
F32 = jnp.float32


def saturation(head, la, n, negp):
    suction = jnp.log(1.0 + jnp.exp2(jnp.abs(head) * (-LOG2E))) + jnp.maximum(-head, 0.0)
    power = jnp.exp2(n * jnp.log(suction) + la)
    return jnp.exp2(negp * jnp.log(1.0 + power))


def pick(row, index):
    parts = []
    for k in range(index.shape[0] // 8):
        parts.append(
            jnp.take_along_axis(row, index[8 * k : 8 * k + 8], axis=1, mode="promise_in_bounds")
        )
    return parts[0] if len(parts) == 1 else jnp.concatenate(parts, axis=0)


def pick_wide(row, index):
    parts = []
    for k in range(index.shape[1] // LANES):
        parts.append(
            jnp.take_along_axis(
                row, index[:, k * LANES : (k + 1) * LANES], axis=1, mode="promise_in_bounds"
            )
        )
    return parts[0] if len(parts) == 1 else jnp.concatenate(parts, axis=1)


def kernel(
    count,
    tiles,
    press,
    old,
    tex,
    zones,
    rates,
    table,
    inverse,
    out,
    old_v,
    tex_v,
    mold_v,
    own,
    halo,
    own2,
    halo2,
    tex_h,
    cond_o,
    cond_h,
    par_o,
    par_h,
    pack_ts,
    pack_tr,
    pack_hs,
    pack_hr,
    col_h,
    col_t,
    col_m,
    par_c,
    cond_c,
    flux_c,
    mis_c,
    zone_v,
    rate_v,
    table_v,
    tab,
    inv_v,
    loc_sem,
    own_sem,
    send_sem,
    recv_sem,
    hsend_sem,
    hrecv_sem,
):
    me = lax.axis_index("layer")
    tile = lax.axis_index("tile")
    rows = press.shape[0]
    width = press.shape[1]
    layers = count * rows // 8
    own_rows = rows // 8
    down = lax.rem(tile + tiles - 1, tiles)
    up = lax.rem(tile + 1, tiles)

    def peer_of(k):
        return lax.rem(me + k, count)

    barrier = pltpu.get_barrier_semaphore()

    def greet(k, carry):
        pl.semaphore_signal(
            barrier, inc=1, device_id={"layer": peer_of(k)}, device_id_type=MESH
        )
        return carry

    lax.fori_loop(1, count, greet, 0)
    pl.semaphore_signal(barrier, inc=1, device_id={"tile": down}, device_id_type=MESH)
    pl.semaphore_signal(barrier, inc=1, device_id={"tile": up}, device_id_type=MESH)

    my_cols = pl.ds(pl.multiple_of(me * LANES, LANES), LANES)
    my_rows = pl.ds(pl.multiple_of(me * rows, rows), rows)
    loads = [
        pltpu.make_async_copy(old, old_v, loc_sem.at[0]),
        pltpu.make_async_copy(tex, tex_v, loc_sem.at[1]),
        pltpu.make_async_copy(table, table_v, loc_sem.at[2]),
        pltpu.make_async_copy(inverse, inv_v, loc_sem.at[3]),
        pltpu.make_async_copy(zones.at[:, my_cols], zone_v, loc_sem.at[4]),
        pltpu.make_async_copy(rates, rate_v, loc_sem.at[5]),
    ]
    for load in loads:
        load.start()
    own_h = pltpu.make_async_copy(press.at[:, my_cols], col_h.at[my_rows], own_sem.at[0])
    own_t = pltpu.make_async_copy(tex.at[:, my_cols], col_t.at[my_rows], own_sem.at[1])
    own_h.start()
    own_t.start()

    def scatter(src, dst, slot):
        def send(k, carry):
            peer = peer_of(k)
            cols = pl.ds(pl.multiple_of(peer * LANES, LANES), LANES)
            pltpu.make_async_remote_copy(
                src_ref=src.at[:, cols],
                dst_ref=dst.at[my_rows],
                send_sem=send_sem.at[slot],
                recv_sem=recv_sem.at[slot],
                device_id={"layer": peer},
                device_id_type=MESH,
            ).start()
            return carry

        lax.fori_loop(1, count, send, 0)

    def arrived(dst, slot):
        part = dst.at[pl.ds(0, (count - 1) * rows)]
        pltpu.make_async_copy(part, part, recv_sem.at[slot]).wait()

    def sent(dst, slot):
        part = dst.at[pl.ds(0, (count - 1) * rows)]
        pltpu.make_async_copy(part, part, send_sem.at[slot]).wait()

    pl.semaphore_wait(barrier, count - 1 + 2)
    scatter(press, col_h, 0)
    scatter(tex, col_t, 1)

    loads[2].wait()
    tab[...] = jnp.ones(tab.shape, F32)
    tab[0:5, 0 : table.shape[1]] = table_v[...]
    t_a, t_n, t_r, t_s, t_k = (tab[j : j + 1, :] for j in range(5))

    def full(row):
        return jnp.broadcast_to(row, (8, LANES))

    tab_la = full(t_n * jnp.log(t_a) * LOG2E)
    tab_n = full(t_n * LOG2E)
    tab_p = full((1.0 / t_n - 1.0) * LOG2E)
    tab_r = full(t_r)
    tab_d = full(t_s - t_r)
    tab_k = full(t_k)

    loads[1].wait()
    for l in range(own_rows):
        pack_ts[0, 2 * l : 2 * l + 2, :] = tex_v[8 * l : 8 * l + 2, :]
        pack_ts[1, 2 * l : 2 * l + 2, :] = tex_v[8 * l + 6 : 8 * l + 8, :]

    def halo_copies(src, dst, slot):
        copies = []
        for side, device in ((0, down), (1, up)):
            copies.append(
                pltpu.make_async_remote_copy(
                    src_ref=src.at[side],
                    dst_ref=dst.at[side],
                    send_sem=hsend_sem.at[slot, side],
                    recv_sem=hrecv_sem.at[slot, side],
                    device_id={"tile": device},
                    device_id_type=MESH,
                )
            )
        return copies

    tex_copies = halo_copies(pack_ts, pack_tr, 0)
    for copy in tex_copies:
        copy.start()

    loads[0].wait()
    chunk = 512
    per_row = width // chunk

    def old_step(i, carry):
        r = pl.ds(pl.multiple_of(lax.div(i, per_row) * 8, 8), 8)
        c = pl.ds(pl.multiple_of(lax.rem(i, per_row) * chunk, chunk), chunk)
        index = tex_v[r, c]
        la, n, negp = pick_wide(tab_la, index), pick_wide(tab_n, index), pick_wide(tab_p, index)
        sat = saturation(old_v[r, c], la, n, negp)
        mold_v[r, c] = pick_wide(tab_r, index) + pick_wide(tab_d, index) * sat
        par_o[0, r, c] = la
        par_o[1, r, c] = n
        par_o[2, r, c] = negp
        par_o[3, r, c] = pick_wide(tab_k, index)
        return carry

    lax.fori_loop(0, own_rows * per_row, old_step, 0)
    scatter(mold_v, col_m, 2)
    own_m = pltpu.make_async_copy(mold_v.at[:, my_cols], col_m.at[my_rows], own_sem.at[2])
    own_m.start()

    for copy in tex_copies:
        copy.wait()
    tex_h[...] = jnp.zeros(tex_h.shape, jnp.int32)
    halo[...] = jnp.zeros(halo.shape, F32)
    for l in range(own_rows):
        tex_h[8 * l : 8 * l + 2, :] = pack_tr[0, 2 * l : 2 * l + 2, :]
        tex_h[8 * l + 6 : 8 * l + 8, :] = pack_tr[1, 2 * l : 2 * l + 2, :]

    def halo_step(i, carry):
        r = pl.ds(pl.multiple_of(lax.div(i, per_row) * 8, 8), 8)
        c = pl.ds(pl.multiple_of(lax.rem(i, per_row) * chunk, chunk), chunk)
        index = tex_h[r, c]
        for j, row in enumerate((tab_la, tab_n, tab_p, tab_k)):
            par_h[j, r, c] = pick_wide(row, index)
        return carry

    lax.fori_loop(0, own_rows * per_row, halo_step, 0)

    block = 64
    blocks = layers * 8 // block
    own_t.wait()
    arrived(col_t, 1)

    def par_step(i, carry):
        r = pl.ds(pl.multiple_of(i * block, block), block)
        index = col_t[r, :]
        for j, row in enumerate((tab_la, tab_n, tab_p, tab_k, tab_r, tab_d)):
            par_c[j, r, :] = pick(row, index)
        return carry

    lax.fori_loop(0, blocks, par_step, 0)
    loads[4].wait()
    loads[5].wait()
    tab[0:1, 0 : rates.shape[1]] = rate_v[...]
    flux_c[0:8, :] = pick(full(tab[0:1, :]), zone_v[...])
    loads[3].wait()
    inv = inv_v[...]
    inv_hi = inv.astype(jnp.bfloat16)
    inv_lo = (inv - inv_hi.astype(F32)).astype(jnp.bfloat16)
    inv_all = jnp.concatenate([inv_hi, inv_lo, inv_hi, inv_lo], axis=1)
    own_h.wait()
    arrived(col_h, 0)

    def closure_step(i, carry):
        r = pl.ds(pl.multiple_of(i * block, block), block)
        sat = saturation(col_h[r, :], par_c[0, r, :], par_c[1, r, :], par_c[2, r, :])
        cond_c[r, :] = par_c[3, r, :] * (sat * sat * sat)
        mis_c[r, :] = sat
        return carry

    def newton(first):
        lax.fori_loop(0, blocks, closure_step, 0)
        if first:
            own_m.wait()
            arrived(col_m, 2)

            def mold_step(i, carry):
                r = pl.ds(pl.multiple_of(i * block, block), block)
                col_m[r, :] = col_m[r, :] - par_c[4, r, :]
                return carry

            lax.fori_loop(0, blocks, mold_step, 0)
        last = layers * 8
        cond_c[last : last + 8, :] = cond_c[last - 8 : last, :]
        col_h[last : last + 8, :] = col_h[last - 8 : last, :]

        def flux_step(i, carry):
            start = pl.multiple_of(i * block, block)
            r = pl.ds(start, block)
            b = pl.ds(pl.multiple_of(start + 8, 8), block)
            below = (0.5 * (cond_c[r, :] + cond_c[b, :])) * (col_h[r, :] - col_h[b, :] + 1.0)
            flux_c[b, :] = below
            above = jnp.concatenate([flux_c[pl.ds(start, 8), :], below[: block - 8]], axis=0)
            moist = par_c[5, r, :] * mis_c[r, :] - col_m[r, :]
            mis_c[r, :] = moist + (below - above)
            return carry

        lax.fori_loop(0, blocks, flux_step, 0)
        for y in range(0, 8, 2):
            x = jnp.concatenate(
                [mis_c[pl.ds(y + j, layers, stride=8), :] for j in range(2)], axis=1
            )
            hi = x.astype(jnp.bfloat16)
            lo = (x - hi.astype(F32)).astype(jnp.bfloat16)
            stacked = jnp.concatenate([hi, hi, lo, lo], axis=0)
            update = jnp.dot(inv_all, stacked, preferred_element_type=F32)
            for j in range(2):
                at = pl.ds(y + j, layers, stride=8)
                col_h[at, :] = col_h[at, :] - update[:, j * LANES : (j + 1) * LANES]

    newton(True)

    def again(i, carry):
        newton(False)
        return carry

    lax.fori_loop(1, ITERS, again, 0)

    own_b = pltpu.make_async_copy(col_h.at[my_rows], own.at[:, my_cols], own_sem.at[3])
    own_b.start()

    def send_back(k, carry):
        peer = peer_of(k)
        pltpu.make_async_remote_copy(
            src_ref=col_h.at[pl.ds(pl.multiple_of(peer * rows, rows), rows)],
            dst_ref=own.at[:, my_cols],
            send_sem=send_sem.at[3],
            recv_sem=recv_sem.at[3],
            device_id={"layer": peer},
            device_id_type=MESH,
        ).start()
        return carry

    lax.fori_loop(1, count, send_back, 0)
    own_b.wait()
    part = own.at[:, pl.ds(0, (count - 1) * LANES)]
    pltpu.make_async_copy(part, part, recv_sem.at[3]).wait()

    for l in range(own_rows):
        pack_hs[0, 2 * l : 2 * l + 2, :] = own[8 * l : 8 * l + 2, :]
        pack_hs[1, 2 * l : 2 * l + 2, :] = own[8 * l + 6 : 8 * l + 8, :]
    head_copies = halo_copies(pack_hs, pack_hr, 1)
    for copy in head_copies:
        copy.start()

    def cond_pass(src, par, dst):
        def step(i, carry):
            r = pl.ds(pl.multiple_of(lax.div(i, per_row) * 8, 8), 8)
            c = pl.ds(pl.multiple_of(lax.rem(i, per_row) * chunk, chunk), chunk)
            sat = saturation(src[r, c], par[0, r, c], par[1, r, c], par[2, r, c])
            dst[r, c] = par[3, r, c] * (sat * sat * sat)
            return carry

        lax.fori_loop(0, own_rows * per_row, step, 0)

    cond_pass(own, par_o, cond_o)
    for copy in head_copies:
        copy.wait()
    for l in range(own_rows):
        halo[8 * l : 8 * l + 2, :] = pack_hr[0, 2 * l : 2 * l + 2, :]
        halo[8 * l + 6 : 8 * l + 8, :] = pack_hr[1, 2 * l : 2 * l + 2, :]

    sub = lax.broadcasted_iota(jnp.int32, (8, width), 0)
    lane = lax.broadcasted_iota(jnp.int32, (8, width), 1)
    right_end = lane == width - 1
    cut_top = jnp.logical_and(sub == 7, tile == tiles - 1)
    cut_bottom = jnp.logical_and(sub == 7, tile == 0)

    def flow(h, c, hn, cn):
        return (0.5 * (c + cn)) * (hn - h)

    def sweep(src_o, src_h, dst_o, dst_h):
        cond_pass(src_h, par_h, cond_h)
        if dst_h is None:
            cond_pass(src_o, par_o, cond_o)

        def step(l, carry):
            r = pl.ds(pl.multiple_of(l * 8, 8), 8)
            h, c, g, e = src_o[r, :], cond_o[r, :], src_h[r, :], cond_h[r, :]

            def next_row(a, b):
                return pltpu.roll(jnp.where(sub == 0, b, a), 7, 0)

            f = jnp.where(cut_top, 0.0, flow(h, c, next_row(h, g), next_row(c, e)))
            fh = jnp.where(cut_bottom, 0.0, flow(g, e, next_row(g, h), next_row(e, c)))

            def across(a, k):
                x = flow(a, k, pltpu.roll(a, width - 1, 1), pltpu.roll(k, width - 1, 1))
                x = jnp.where(right_end, 0.0, x)
                return x - pltpu.roll(x, 1, 1)

            change = f - pltpu.roll(jnp.where(sub == 7, fh, f), 1, 0) + across(h, c)
            dst_o[r, :] = h + OMEGA * change
            if dst_h is not None:
                change = fh - pltpu.roll(jnp.where(sub == 7, f, fh), 1, 0) + across(g, e)
                dst_h[r, :] = g + OMEGA * change
            return carry

        lax.fori_loop(0, own_rows, step, 0)

    sweep(own, halo, own2, halo2)
    sweep(own2, halo2, own, None)
    store = pltpu.make_async_copy(own, out, own_sem.at[4])
    store.start()
    sent(col_h, 0)
    sent(col_t, 1)
    sent(col_m, 2)
    sent(col_h, 3)
    store.wait()


def body(pressure, old_pressure, texture, zones, rates, vg_table, approx_inverse):
    count = lax.axis_size("layer")
    tiles = lax.axis_size("tile")
    depth, tall, width = pressure.shape
    rows = depth * tall
    total = rows * count
    flat = (rows, width)

    def vmem(*shape, dtype=F32):
        return pltpu.VMEM(shape, dtype)

    result = pl.pallas_call(
        functools.partial(kernel, count, tiles),
        out_shape=jax.ShapeDtypeStruct(flat, F32),
        in_specs=[pl.BlockSpec(memory_space=pl.ANY)] * 7,
        out_specs=pl.BlockSpec(memory_space=pl.ANY),
        scratch_shapes=[
            vmem(*flat),
            vmem(*flat, dtype=jnp.int32),
            vmem(*flat),
            vmem(*flat),
            vmem(*flat),
            vmem(*flat),
            vmem(*flat),
            vmem(*flat, dtype=jnp.int32),
            vmem(*flat),
            vmem(*flat),
            vmem(4, *flat),
            vmem(4, *flat),
            vmem(2, 2 * depth, width, dtype=jnp.int32),
            vmem(2, 2 * depth, width, dtype=jnp.int32),
            vmem(2, 2 * depth, width),
            vmem(2, 2 * depth, width),
            vmem(total + 8, LANES),
            vmem(total, LANES, dtype=jnp.int32),
            vmem(total, LANES),
            vmem(6, total, LANES),
            vmem(total + 8, LANES),
            vmem(total + 8, LANES),
            vmem(total, LANES),
            vmem(tall, LANES, dtype=jnp.int32),
            vmem(1, rates.shape[0]),
            vmem(*vg_table.shape),
            vmem(8, LANES),
            vmem(*approx_inverse.shape),
            pltpu.SemaphoreType.DMA((6,)),
            pltpu.SemaphoreType.DMA((5,)),
            pltpu.SemaphoreType.DMA((4,)),
            pltpu.SemaphoreType.DMA((4,)),
            pltpu.SemaphoreType.DMA((2, 2)),
            pltpu.SemaphoreType.DMA((2, 2)),
        ],
        compiler_params=pltpu.CompilerParams(
            collective_id=0, has_side_effects=True, vmem_limit_bytes=48 * 1024 * 1024
        ),
    )(
        pressure.reshape(flat),
        old_pressure.reshape(flat),
        texture.reshape(flat),
        zones,
        rates.reshape(1, -1),
        vg_table,
        approx_inverse,
    )
    return result.reshape(pressure.shape)


def solution(mesh):
    placed = (
        P("layer", "tile", None),
        P("layer", "tile", None),
        P("layer", "tile", None),
        P("tile", None),
        P(),
        P(),
        P(),
    )
    return jax.shard_map(
        body, mesh=mesh, in_specs=placed, out_specs=P("layer", "tile", None), check_vma=False
    )
```

time: 492 us -> 57.7 us (0.12); the launches traced: 484 us -> 56.7 us
  waiting for transfers between devices: 329 us -> 0 us
  other arithmetic: 60.3 us -> 0 us
  Pallas kernels: 0 us -> 50.9 us
  starting transfers between devices: 43.8 us -> 0 us
  matrix products: 24.5 us -> 0 us
  between operations: 13.8 us -> 0.02 us
  local copies, waits for them, and re-layouts: 12.8 us -> 5.84 us
    all_gather x3 -> x0, waiting for transfers between devices: 309 us -> none  [body(): piece = lax.all_gather(misfit, 'layer', axis=0, tiled=True)]
    pallas_call x0 -> x1, Pallas kernels: none -> 50.9 us  [body(): pl.pallas_call(functools.partial(kernel, count, tiles), out_shape=jax.Sha...]
    ppermute x10 -> x0, starting transfers between devices: 43 us -> none  [the longest x5 27.8 us: with_halo(): lax.ppermute(lax.slice_in_dim(block, 0, width, axis=dim), axis, backward)]
    mul x11 -> x0, other arithmetic: 32.7 us -> none  [the longest x2 30.3 us: closures(): conduct = saturated_k * saturation * saturation * saturation]
    dot_general x3 -> x0, matrix products: 24.5 us -> none  [body(): jnp.dot(block, piece.reshape(piece.shape[0], -1), precision=lax.Precision...]
    add x4 -> x0, other arithmetic: 23.9 us -> none  [the longest x3 23.6 us: body(): misfit = (moisture - moisture_old) / DT + (fluxes[1:] - fluxes[:-1]) / DZ]
    ppermute x10 -> x0, waiting for transfers between devices: 20.2 us -> none  [the longest x5 17.8 us: with_halo(): lax.ppermute(lax.slice_in_dim(block, 0, width, axis=dim), axis, backward)]
    slice x7 -> x0, local copies, waits for them, and re-layouts: 7.87 us -> none  [the longest x4 7.77 us: lookup(): total = total + jnp.where(texture == klass, vg_table[row, klass], 0.0)]
  transfers between devices with their start and end apart: 13 -> 0, of which waited for: 10 -> 0; matrix products, arithmetic and copies ran while one was open for 1% -> 0% of each run, Pallas kernels for 0% -> 0%
where the time goes in v1:
time: 57.7 us; the launch traced here: 56.7 us
  Pallas kernels  50.9 us (88%)
  local copies, waits for them, and re-layouts  5.84 us (10%)
    pallas_call x1, Pallas kernels, body(): pl.pallas_call(functools.partial(kernel, count, tiles), out_shape=jax.Sha...  50.9 us
    unnamed x15, local copies, waits for them, and re-layouts  5.84 us

profile of v1, /device:TPU:56, one launch (start us, length us, event | category | flops | bytes accessed | tf_op | source)
XLA Modules:
  0.0 56.7 jit_solution(2411357893699171959)
XLA Ops:
  0.0 0.0 copy-start.5
  0.0 0.0 copy-start.6
  0.0 0.7 %copy-done.5 = f32[5,12]{1,0:T(8,128)S(1)} copy-done((f32[5,12]{1,0:T(8,128)S(1)}, f32[5,12]{1,0:T(8,128)}, u32[]{:S(2)}) %copy-start.5) | copy-done | bytes 264
  0.7 0.0 copy-done.6
  0.7 0.0 copy-start
  0.7 0.9 %copy-done = f32[4,8,2048]{2,1,0:T(8,128)S(1)} copy-done((f32[4,8,2048]{2,1,0:T(8,128)S(1)}, f32[4,8,2048]{2,1,0:T(8,128)}, u32[]{:S(2)}) %copy-start) | copy-done | bytes 262168
  1.6 0.0 copy-start.1
  1.6 0.9 %copy-done.1 = f32[4,8,2048]{2,1,0:T(8,128)S(1)} copy-done((f32[4,8,2048]{2,1,0:T(8,128)S(1)}, f32[4,8,2048]{2,1,0:T(8,128)}, u32[]{:S(2)}) %copy-start.1) | copy-done | bytes 262168
  2.6 0.0 copy-start.2
  2.6 0.9 %copy-done.2 = s32[4,8,2048]{2,1,0:T(8,128)S(1)} copy-done((s32[4,8,2048]{2,1,0:T(8,128)S(1)}, s32[4,8,2048]{2,1,0:T(8,128)}, u32[]{:S(2)}) %copy-start.2) | copy-done | bytes 262168
  3.5 0.0 copy-start.3
  3.5 0.8 %copy-done.3 = s32[8,2048]{1,0:T(8,128)S(1)} copy-done((s32[8,2048]{1,0:T(8,128)S(1)}, s32[8,2048]{1,0:T(8,128)}, u32[]{:S(2)}) %copy-start.3) | copy-done | bytes 65560
  4.4 0.0 copy-start.4
  4.4 0.8 %copy-done.4 = f32[64,64]{1,0:T(8,128)S(1)} copy-done((f32[64,64]{1,0:T(8,128)S(1)}, f32[64,64]{1,0:T(8,128)}, u32[]{:S(2)}) %copy-start.4) | copy-done | bytes 16408
  5.1 50.9 %shard_map.73 = f32[32,2048]{1,0:T(8,128)S(1)} custom-call(f32[32,2048]{1,0:T(8,128)S(1)} %bitcast.6, f32[32,2048]{1,0:T(8,128)S(1)} %bitcast.7, s32[32,2048]{1,0:T(8,128)S(1)} %bitcast.8, s32[8,2048]{1,0:T(8,128)S(1)} %copy-done.3, f32[1,16]{1,0:T(1,128)S(1)} %bitcast.9, f32[5,12]{1,0:T(8,128)S(1)} %copy-done.5, f32[64,64]{1,0:T(8,128)S(1)} %copy-done.4), custom_call_target="tpu_custom_call" | custom-call | tf_op jit(solution)/shard_map/pallas_call | solution.py:423
  56.0 0.7 %copy.9 = f32[4,8,2048]{2,1,0:T(8,128)} copy(f32[4,8,2048]{2,1,0:T(8,128)S(1)} %bitcast.5) | data formatting | bytes 524288
Async XLA Ops:
  0.0 0.7 %copy-start.5 = (f32[5,12]{1,0:T(8,128)S(1)}, f32[5,12]{1,0:T(8,128)}, u32[]{:S(2)}) copy-start(f32[5,12]{1,0:T(8,128)} %table.1) | copy-start | bytes 724
  0.0 0.7 %copy-start.6 = (f32[16]{0:T(128)S(1)}, f32[16]{0:T(128)}, u32[]{:S(2)}) copy-start(f32[16]{0:T(128)} %param.11) | copy-start | bytes 196
  0.7 1.0 %copy-start = (f32[4,8,2048]{2,1,0:T(8,128)S(1)}, f32[4,8,2048]{2,1,0:T(8,128)}, u32[]{:S(2)}) copy-start(f32[4,8,2048]{2,1,0:T(8,128)} %param.7) | copy-start | bytes 786436
  1.6 0.9 %copy-start.1 = (f32[4,8,2048]{2,1,0:T(8,128)S(1)}, f32[4,8,2048]{2,1,0:T(8,128)}, u32[]{:S(2)}) copy-start(f32[4,8,2048]{2,1,0:T(8,128)} %param.8) | copy-start | bytes 786436
  2.6 0.9 %copy-start.2 = (s32[4,8,2048]{2,1,0:T(8,128)S(1)}, s32[4,8,2048]{2,1,0:T(8,128)}, u32[]{:S(2)}) copy-start(s32[4,8,2048]{2,1,0:T(8,128)} %param.9) | copy-start | bytes 786436
  3.5 0.8 %copy-start.3 = (s32[8,2048]{1,0:T(8,128)S(1)}, s32[8,2048]{1,0:T(8,128)}, u32[]{:S(2)}) copy-start(s32[8,2048]{1,0:T(8,128)} %zones.1) | copy-start | bytes 196612
  4.4 0.8 %copy-start.4 = (f32[64,64]{1,0:T(8,128)S(1)}, f32[64,64]{1,0:T(8,128)}, u32[]{:S(2)}) copy-start(f32[64,64]{1,0:T(8,128)} %inverse.1) | copy-start | bytes 49156

commit v2 on v0

v2 whole, which is shorter than its diff:
```python
import functools

import jax
import jax.numpy as jnp
from jax import lax
from jax.experimental import pallas as pl
from jax.experimental.pallas import tpu as pltpu
from jax.sharding import PartitionSpec as P

ITERS = 3
OMEGA = 0.2
LOG2E = 1.4426950408889634
MESH = pl.DeviceIdType.MESH
LANES = 128
CHUNKS = 4
FIELDS = 3
F32 = jnp.float32


def saturation(head, la, n, negp):
    suction = jnp.log(1.0 + jnp.exp2(jnp.abs(head) * (-LOG2E))) + jnp.maximum(-head, 0.0)
    power = jnp.exp2(n * jnp.log(suction) + la)
    return jnp.exp2(negp * jnp.log(1.0 + power))


def exchange(tiles):
    sub = lax.broadcasted_iota(jnp.int32, tiles[0].shape, 0)
    low, even = sub < 4, (sub & 2) == 0
    a, b, c, d = tiles

    def halves(p, q):
        r = pltpu.roll(jnp.where(low, q, p), 4, 0)
        return jnp.where(low, p, r), jnp.where(low, r, q)

    def pairs(p, q):
        return (
            jnp.where(even, p, pltpu.roll(q, 2, 0)),
            jnp.where(even, pltpu.roll(p, 6, 0), q),
        )

    a, c = halves(a, c)
    b, d = halves(b, d)
    a, b = pairs(a, b)
    c, d = pairs(c, d)
    return a, b, c, d


def lookup(splat, classes, row, index, masks):
    def constant(k):
        tile = splat[row, min(k, classes - 1)]
        if len(index.shape) == 2:
            return jnp.concatenate([tile] * (index.shape[1] // LANES), axis=1)
        return jnp.broadcast_to(tile[None], index.shape)

    level = [constant(k) for k in range(classes)]
    for mask in masks:
        level = [
            jnp.where(mask, level[k + 1], level[k]) if k + 1 < len(level) else level[k]
            for k in range(0, len(level), 2)
        ]
    return level[0]


def bits(index, classes):
    return [(index & (1 << b)) != 0 for b in range((classes - 1).bit_length())]


def kernel(
    count,
    tiles,
    press,
    old,
    tex,
    zones,
    rates,
    table,
    inverse,
    out,
    nat_h,
    nat_o,
    nat_t,
    stage,
    colb,
    hcur,
    par_c,
    mold_c,
    mis_c,
    upd_c,
    ghost,
    lay,
    lay2,
    cond,
    swap_h,
    swap_c,
    par_l,
    tex_h,
    fin,
    zone_v,
    rate_v,
    table_v,
    tab,
    splat,
    inv_v,
    load_sem,
    in_send,
    in_recv,
    back_send,
    back_recv,
    halo_send,
    halo_recv,
    tex_send,
    tex_recv,
):
    me = lax.axis_index("layer")
    tile = lax.axis_index("tile")
    width = press.shape[1]
    depth = press.shape[0] // 8
    classes = table.shape[1]
    layers = count * depth
    down = lax.rem(tile + tiles - 1, tiles)
    up = lax.rem(tile + 1, tiles)
    wide = 512
    blocks = width // wide

    def peer_of(k):
        return lax.rem(me + k, count)

    def greet(k, carry):
        pl.semaphore_signal(
            pltpu.get_barrier_semaphore(),
            inc=1,
            device_id={"layer": peer_of(k)},
            device_id_type=MESH,
        )
        return carry

    def greet_down(k, carry):
        pl.semaphore_signal(
            pltpu.get_barrier_semaphore(),
            inc=1,
            device_id={"tile": down, "layer": peer_of(k)},
            device_id_type=MESH,
        )
        return carry

    lax.fori_loop(1, count, greet, 0)
    lax.fori_loop(0, count, greet_down, 0)

    my_cols = pl.ds(pl.multiple_of(me * LANES, LANES), LANES)
    loads = [
        pltpu.make_async_copy(table, table_v, load_sem.at[0]),
        pltpu.make_async_copy(press, nat_h, load_sem.at[1]),
        pltpu.make_async_copy(old, nat_o, load_sem.at[2]),
        pltpu.make_async_copy(tex, nat_t, load_sem.at[3]),
        pltpu.make_async_copy(inverse, inv_v, load_sem.at[4]),
        pltpu.make_async_copy(zones.at[:, my_cols], zone_v, load_sem.at[5]),
        pltpu.make_async_copy(rates, rate_v, load_sem.at[6]),
    ]
    for load in loads:
        load.start()

    loads[0].wait()
    tab[...] = jnp.ones(tab.shape, F32)
    tab[0:5, 0:classes] = table_v[...]
    t_a, t_n, t_r, t_s, t_k = (tab[j : j + 1, :] for j in range(5))
    derived = (
        t_n * jnp.log(t_a) * LOG2E,
        t_n * LOG2E,
        (1.0 / t_n - 1.0) * LOG2E,
        t_k,
        t_r,
        t_s - t_r,
    )
    for j, row in enumerate(derived):
        for k in range(classes):
            splat[j, k] = jnp.broadcast_to(row[:, k : k + 1], (8, LANES))

    for load in loads[1:4]:
        load.wait()

    def pack(b, carry):
        cols = pl.ds(pl.multiple_of(b * wide, wide), wide)
        for f, nat in enumerate((nat_h, nat_o, nat_t)):
            rows = [nat[8 * l : 8 * l + 8, cols] for l in range(depth)]
            if f == 2:
                rows = [r.astype(F32) for r in rows]
            for c, packed in enumerate(exchange(rows)):
                stage[c, 8 * f : 8 * f + 8, cols] = packed
        return carry

    lax.fori_loop(0, blocks, pack, 0)

    def params_of(texture, slot):
        def step(b, carry):
            cols = pl.ds(pl.multiple_of(b * wide, wide), wide)
            index = texture(cols).astype(jnp.int32)
            masks = bits(index, classes)
            for j in range(4):
                par_l[j, slot, :, cols] = lookup(splat, classes, j, index, masks)
            return carry

        lax.fori_loop(0, blocks, step, 0)

    for c in range(CHUNKS):
        params_of(lambda cols, c=c: stage[c, 16:24, cols], c + 1)

    pl.semaphore_wait(pltpu.get_barrier_semaphore(), count - 1 + count)

    order = (3, 0, 1, 2)
    for c in order:

        def send(k, carry, c=c):
            peer = peer_of(k)
            pltpu.make_async_remote_copy(
                src_ref=stage.at[c, :, pl.ds(pl.multiple_of(peer * LANES, LANES), LANES)],
                dst_ref=colb.at[c, me],
                send_sem=in_send.at[c],
                recv_sem=in_recv.at[c],
                device_id={"layer": peer},
                device_id_type=MESH,
            ).start()
            return carry

        lax.fori_loop(1, count, send, 0)
        if c == 3:
            tex_up = pltpu.make_async_remote_copy(
                src_ref=stage.at[3, pl.ds(16, 8)],
                dst_ref=tex_h.at[0],
                send_sem=tex_send.at[0],
                recv_sem=tex_recv.at[0],
                device_id={"tile": up},
                device_id_type=MESH,
            )
            tex_up.start()
        colb[c, me] = stage[c, :, my_cols]

    loads[5].wait()
    loads[6].wait()
    tab[0:1, 0 : rates.shape[1]] = rate_v[...]
    inflow = jnp.take_along_axis(
        jnp.broadcast_to(tab[0:1, :], (8, LANES)), zone_v[...], axis=1, mode="promise_in_bounds"
    )
    for c in range(CHUNKS):
        ghost[c] = pltpu.roll(inflow, (6 - 2 * c) % 8, 0)

    loads[4].wait()
    inv = inv_v[...]
    inv_hi = inv.astype(jnp.bfloat16)
    inv_lo = (inv - inv_hi.astype(F32)).astype(jnp.bfloat16)
    inv_all = jnp.concatenate([inv_hi, inv_lo, inv_hi], axis=1)

    shape = (count, 8, LANES)
    sub3 = lax.broadcasted_iota(jnp.int32, shape, 1)

    def below(x):
        last = pltpu.roll(x[count - 1 :], 2, 1)
        return pltpu.roll(jnp.where(sub3 < 2, jnp.concatenate([x[1:], last], axis=0), x), 6, 1)

    def newton(c):
        group = 4

        def params(g, carry):
            at = pl.ds(g * group, group)
            index = colb[c, at, 16:24, :].astype(jnp.int32)
            masks = bits(index, classes)
            values = [lookup(splat, classes, j, index, masks) for j in range(6)]
            for j in range(6):
                par_c[j, at] = values[j]
            sat = saturation(colb[c, at, 8:16, :], values[0], values[1], values[2])
            mold_c[at] = values[4] + values[5] * sat
            return carry

        lax.fori_loop(0, count // group, params, 0)
        hcur[c] = colb[c, :, 0:8, :].reshape(count * 8, LANES)

        def step(i, carry):
            h = hcur[c].reshape(shape)
            sat = saturation(h, par_c[0], par_c[1], par_c[2])
            k = par_c[3] * (sat * sat * sat)
            flux = (0.5 * (k + below(k))) * (h - below(h) + 1.0)
            shifted = jnp.concatenate([ghost[c][None], flux[:-1]], axis=0)
            above = pltpu.roll(jnp.where(sub3 >= 6, shifted, flux), 2, 1)
            moisture = par_c[4] + par_c[5] * sat
            misfit = (moisture - mold_c[...]) + (flux - above)
            mis_c[...] = misfit.reshape(count * 8, LANES)
            x = jnp.concatenate(
                [mis_c[pl.ds(y, layers, stride=2), :] for y in range(2)], axis=1
            )
            hi = x.astype(jnp.bfloat16)
            lo = (x - hi.astype(F32)).astype(jnp.bfloat16)
            stacked = jnp.concatenate([hi, hi, lo], axis=0)
            update = jnp.dot(inv_all, stacked, preferred_element_type=F32)
            for y in range(2):
                upd_c[pl.ds(y, layers, stride=2), :] = update[:, y * LANES : (y + 1) * LANES]
            hcur[c] = hcur[c] - upd_c[...]
            return carry

        lax.fori_loop(0, ITERS, step, 0)

    def tile_rows(peer):
        return pl.ds(pl.multiple_of(peer * 8, 8), 8)

    def send_halo(c, slot, side, device):
        def send(k, carry):
            peer = peer_of(k)
            pltpu.make_async_remote_copy(
                src_ref=hcur.at[c, tile_rows(peer)],
                dst_ref=lay.at[slot, :, my_cols],
                send_sem=halo_send.at[side],
                recv_sem=halo_recv.at[side],
                device_id={"tile": device, "layer": peer},
                device_id_type=MESH,
            ).start()
            return carry

        lax.fori_loop(0, count, send, 0)

    def send_back(c):
        def send(k, carry):
            peer = peer_of(k)
            pltpu.make_async_remote_copy(
                src_ref=hcur.at[c, tile_rows(peer)],
                dst_ref=lay.at[c + 1, :, my_cols],
                send_sem=back_send.at[c],
                recv_sem=back_recv.at[c],
                device_id={"layer": peer},
                device_id_type=MESH,
            ).start()
            return carry

        lax.fori_loop(1, count, send, 0)
        lay[c + 1, :, my_cols] = hcur[c, tile_rows(me), :]

    for c in order:
        part = colb.at[c, pl.ds(0, count - 1)]
        pltpu.make_async_copy(part, part, in_recv.at[c]).wait()
        newton(c)
        if c == 3:
            send_halo(3, 0, 0, up)
        send_back(c)

    tex_up.wait_recv()
    tex_down = pltpu.make_async_remote_copy(
        src_ref=stage.at[0, pl.ds(16, 8)],
        dst_ref=tex_h.at[1],
        send_sem=tex_send.at[1],
        recv_sem=tex_recv.at[1],
        device_id={"tile": down},
        device_id_type=MESH,
    )
    tex_down.start()
    send_halo(0, 5, 1, down)
    params_of(lambda cols: tex_h[0, :, cols], 0)

    def odd_rows(shape):
        return (lax.broadcasted_iota(jnp.int32, shape, 0) & 1) == 1

    def prepare(src, s):
        def step(b, carry):
            cols = pl.ds(pl.multiple_of(b * wide, wide), wide)
            h = src[s, :, cols]
            sat = saturation(h, par_l[0, s, :, cols], par_l[1, s, :, cols], par_l[2, s, :, cols])
            k = par_l[3, s, :, cols] * (sat * sat * sat)
            odd = odd_rows(h.shape)
            cond[s, :, cols] = k
            swap_h[s, :, cols] = jnp.where(odd, pltpu.roll(h, 1, 0), pltpu.roll(h, 7, 0))
            swap_c[s, :, cols] = jnp.where(odd, pltpu.roll(k, 1, 0), pltpu.roll(k, 7, 0))
            return carry

        lax.fori_loop(0, blocks, step, 0)

    def advance(src, dst, s):
        h, k = src[s], cond[s]
        lane = lax.broadcasted_iota(jnp.int32, h.shape, 1)
        flow = (k + pltpu.roll(k, width - 1, 1)) * (pltpu.roll(h, width - 1, 1) - h)
        flow = jnp.where(lane == width - 1, 0.0, flow)
        change = flow - pltpu.roll(flow, 1, 1)
        change = change + (k + swap_c[s]) * (swap_h[s] - h)
        odd = odd_rows(h.shape)
        after, before = min(s + 1, CHUNKS + 1), max(s - 1, 0)
        side_h = jnp.where(odd, swap_h[after], swap_h[before])
        side_c = jnp.where(odd, swap_c[after], swap_c[before])
        side = (k + side_c) * (side_h - h)
        if s == 1:
            side = jnp.where(jnp.logical_and(tile == 0, jnp.logical_not(odd)), 0.0, side)
        if s == CHUNKS:
            side = jnp.where(jnp.logical_and(tile == tiles - 1, odd), 0.0, side)
        dst[s] = h + (0.5 * OMEGA) * (change + side)

    for c in order:
        part = lay.at[c + 1, :, pl.ds(0, (count - 1) * LANES)]
        pltpu.make_async_copy(part, part, back_recv.at[c]).wait()
        prepare(lay, c + 1)
    tex_down.wait_recv()
    params_of(lambda cols: tex_h[1, :, cols], 5)
    pltpu.make_async_copy(lay.at[5], lay.at[5], halo_recv.at[1]).wait()
    prepare(lay, 5)
    for s in (2, 3, 4, 5):
        advance(lay, lay2, s)
    pltpu.make_async_copy(lay.at[0], lay.at[0], halo_recv.at[0]).wait()
    prepare(lay, 0)
    for s in (0, 1):
        advance(lay, lay2, s)
    for s in range(6):
        prepare(lay2, s)
    for s in (1, 2, 3, 4):
        advance(lay2, fin, s)

    def unpack(b, carry):
        cols = pl.ds(pl.multiple_of(b * wide, wide), wide)
        for l, rows in enumerate(exchange([fin[c + 1, :, cols] for c in range(CHUNKS)])):
            nat_h[8 * l : 8 * l + 8, cols] = rows
        return carry

    lax.fori_loop(0, blocks, unpack, 0)
    store = pltpu.make_async_copy(nat_h, out, load_sem.at[7])
    store.start()
    for c in range(CHUNKS):
        part = colb.at[c, pl.ds(0, count - 1)]
        pltpu.make_async_copy(part, part, in_send.at[c]).wait()
        part = hcur.at[c, pl.ds(0, (count - 1) * 8)]
        pltpu.make_async_copy(part, part, back_send.at[c]).wait()
    pltpu.make_async_copy(hcur.at[3], hcur.at[3], halo_send.at[0]).wait()
    pltpu.make_async_copy(hcur.at[0], hcur.at[0], halo_send.at[1]).wait()
    tex_up.wait_send()
    tex_down.wait_send()
    store.wait()


def body(pressure, old_pressure, texture, zones, rates, vg_table, approx_inverse):
    count = lax.axis_size("layer")
    tiles = lax.axis_size("tile")
    depth, tall, width = pressure.shape
    rows = depth * tall
    flat = (rows, width)
    slots = (CHUNKS + 2, 2 * depth, width)
    column = (count, 2 * depth, LANES)
    classes = vg_table.shape[1]

    def vmem(*shape, dtype=F32):
        return pltpu.VMEM(shape, dtype)

    result = pl.pallas_call(
        functools.partial(kernel, count, tiles),
        out_shape=jax.ShapeDtypeStruct(flat, F32),
        in_specs=[pl.BlockSpec(memory_space=pltpu.HBM)] * 7,
        out_specs=pl.BlockSpec(memory_space=pltpu.HBM),
        scratch_shapes=[
            vmem(*flat),
            vmem(*flat),
            vmem(*flat, dtype=jnp.int32),
            vmem(CHUNKS, FIELDS * 2 * depth, width),
            vmem(CHUNKS, count, FIELDS * 2 * depth, LANES),
            vmem(CHUNKS, count * 2 * depth, LANES),
            vmem(6, *column),
            vmem(*column),
            vmem(count * 2 * depth, LANES),
            vmem(count * 2 * depth, LANES),
            vmem(CHUNKS, 8, LANES),
            vmem(*slots),
            vmem(*slots),
            vmem(*slots),
            vmem(*slots),
            vmem(*slots),
            vmem(4, *slots),
            vmem(2, 2 * depth, width),
            vmem(*slots),
            vmem(tall, LANES, dtype=jnp.int32),
            vmem(1, rates.shape[0]),
            vmem(*vg_table.shape),
            vmem(8, LANES),
            vmem(6, classes, 8, LANES),
            vmem(*approx_inverse.shape),
            pltpu.SemaphoreType.DMA((8,)),
            pltpu.SemaphoreType.DMA((CHUNKS,)),
            pltpu.SemaphoreType.DMA((CHUNKS,)),
            pltpu.SemaphoreType.DMA((CHUNKS,)),
            pltpu.SemaphoreType.DMA((CHUNKS,)),
            pltpu.SemaphoreType.DMA((2,)),
            pltpu.SemaphoreType.DMA((2,)),
            pltpu.SemaphoreType.DMA((2,)),
            pltpu.SemaphoreType.DMA((2,)),
        ],
        compiler_params=pltpu.CompilerParams(
            collective_id=0, has_side_effects=True, vmem_limit_bytes=56 * 1024 * 1024
        ),
    )(
        pressure.reshape(flat),
        old_pressure.reshape(flat),
        texture.reshape(flat),
        zones,
        rates.reshape(1, -1),
        vg_table,
        approx_inverse,
    )
    return result.reshape(pressure.shape)


def solution(mesh):
    placed = (
        P("layer", "tile", None),
        P("layer", "tile", None),
        P("layer", "tile", None),
        P("tile", None),
        P(),
        P(),
        P(),
    )
    return jax.shard_map(
        body, mesh=mesh, in_specs=placed, out_specs=P("layer", "tile", None), check_vma=False
    )
```

time: 492 us -> 44.1 us (0.09)
  the two profiles are of different devices: /device:TPU:56 before, /device:TPU:385 now
where the time goes in v2:
time: 44.1 us; the launch traced here: 43.9 us
  Pallas kernels  42.2 us (96%)
  local copies, waits for them, and re-layouts  1.67 us (4%)
    pallas_call x1, Pallas kernels, body(): pl.pallas_call(functools.partial(kernel, count, tiles), out_shape=jax.Sha...  42.2 us
    unnamed x1, local copies, waits for them, and re-layouts  1.67 us

profile of v2, /device:TPU:385, one launch (start us, length us, event | category | flops | bytes accessed | tf_op | source)
XLA Modules:
  0.0 43.9 jit_solution(7915049453574404280)
XLA Ops:
  0.0 42.2 %shard_map.73 = f32[32,2048]{1,0:T(8,128)} custom-call(f32[32,2048]{1,0:T(8,128)} %bitcast.6, f32[32,2048]{1,0:T(8,128)} %bitcast.7, s32[32,2048]{1,0:T(8,128)} %bitcast.8, s32[8,2048]{1,0:T(8,128)} %zones.1, f32[1,16]{1,0:T(1,128)} %bitcast.9, f32[5,12]{1,0:T(8,128)} %table.1, f32[64,64]{1,0:T(8,128)} %inverse.1), custom_call_target="tpu_custom_call" | custom-call | tf_op jit(solution)/shard_map/pallas_call | solution.py:443
  42.2 1.7 %copy.9 = f32[4,8,2048]{2,1,0:T(8,128)} copy(f32[4,8,2048]{2,1,0:T(8,128)} %bitcast.5) | data formatting | bytes 524288

commit v3 on v2

--- a/solution.py
+++ b/solution.py
@@ -14,6 +14,8 @@
 LANES = 128
 CHUNKS = 4
 FIELDS = 3
+GROUPS = ((3, 0), (1, 2))
+ORDER = sum(GROUPS, ())
 F32 = jnp.float32
 
 
@@ -80,7 +82,8 @@
     nat_o,
     nat_t,
     stage,
-    colb,
+    colb_a,
+    colb_b,
     hcur,
     par_c,
     mold_c,
@@ -89,9 +92,8 @@
     ghost,
     lay,
     lay2,
-    cond,
-    swap_h,
-    swap_c,
+    ready,
+    ready2,
     par_l,
     tex_h,
     fin,
@@ -111,6 +113,7 @@
     tex_send,
     tex_recv,
 ):
+    colb = (colb_a, colb_b)
     me = lax.axis_index("layer")
     tile = lax.axis_index("tile")
     width = press.shape[1]
@@ -125,26 +128,30 @@
     def peer_of(k):
         return lax.rem(me + k, count)
 
+    run = tiles // 2
+    above, beneath = tile != tiles - 1, tile != 0
+    last, first = tile == run - 1, tile == run
+    greets_up = jnp.logical_and(above, jnp.logical_not(last))
+    greeted_below = jnp.logical_and(beneath, jnp.logical_not(first))
+
+    def hello(device):
+        pl.semaphore_signal(
+            pltpu.get_barrier_semaphore(), inc=1, device_id=device, device_id_type=MESH
+        )
+
     def greet(k, carry):
-        pl.semaphore_signal(
-            pltpu.get_barrier_semaphore(),
-            inc=1,
-            device_id={"layer": peer_of(k)},
-            device_id_type=MESH,
-        )
+        hello({"layer": peer_of(k)})
         return carry
 
-    def greet_down(k, carry):
-        pl.semaphore_signal(
-            pltpu.get_barrier_semaphore(),
-            inc=1,
-            device_id={"tile": down, "layer": peer_of(k)},
-            device_id_type=MESH,
-        )
-        return carry
-
     lax.fori_loop(1, count, greet, 0)
-    lax.fori_loop(0, count, greet_down, 0)
+
+    @pl.when(greets_up)
+    def _():
+        hello({"tile": up})
+
+    @pl.when(first)
+    def _():
+        hello({"tile": down})
 
     my_cols = pl.ds(pl.multiple_of(me * LANES, LANES), LANES)
     loads = [
@@ -185,10 +192,13 @@
             if f == 2:
                 rows = [r.astype(F32) for r in rows]
             for c, packed in enumerate(exchange(rows)):
-                stage[c, 8 * f : 8 * f + 8, cols] = packed
+                stage[pl.ds(ORDER.index(c) * FIELDS * 8 + 8 * f, 8), cols] = packed
         return carry
 
     lax.fori_loop(0, blocks, pack, 0)
+
+    def at_stage(c):
+        return ORDER.index(c) * FIELDS * 8
 
     def params_of(texture, slot):
         def step(b, carry):
@@ -202,37 +212,46 @@
         lax.fori_loop(0, blocks, step, 0)
 
     for c in range(CHUNKS):
-        params_of(lambda cols, c=c: stage[c, 16:24, cols], c + 1)
-
-    pl.semaphore_wait(pltpu.get_barrier_semaphore(), count - 1 + count)
-
-    order = (3, 0, 1, 2)
-    for c in order:
-
-        def send(k, carry, c=c):
+        params_of(lambda cols, c=c: stage[pl.ds(at_stage(c) + 16, 8), cols], c + 1)
+
+    greeted = count - 1 + jnp.where(greeted_below, 1, 0) + jnp.where(last, 1, 0)
+    pl.semaphore_wait(pltpu.get_barrier_semaphore(), greeted)
+
+    def beside(side):
+        return pltpu.make_async_remote_copy(
+            src_ref=stage.at[pl.ds(at_stage(3 if side == 0 else 0) + 16, 8)],
+            dst_ref=tex_h.at[side],
+            send_sem=tex_send.at[side],
+            recv_sem=tex_recv.at[side],
+            device_id={"tile": up if side == 0 else down},
+            device_id_type=MESH,
+        )
+
+    @pl.when(greeted_below)
+    def _():
+        beside(1).start()
+
+    @pl.when(last)
+    def _():
+        beside(0).start()
+
+    for g, chunks in enumerate(GROUPS):
+        rows = pl.ds(at_stage(chunks[0]), len(chunks) * FIELDS * 8)
+
+        def send_in(k, carry, g=g, rows=rows):
             peer = peer_of(k)
             pltpu.make_async_remote_copy(
-                src_ref=stage.at[c, :, pl.ds(pl.multiple_of(peer * LANES, LANES), LANES)],
-                dst_ref=colb.at[c, me],
-                send_sem=in_send.at[c],
-                recv_sem=in_recv.at[c],
+                src_ref=stage.at[rows, pl.ds(pl.multiple_of(peer * LANES, LANES), LANES)],
+                dst_ref=colb[g].at[me],
+                send_sem=in_send.at[g],
+                recv_sem=in_recv.at[g],
                 device_id={"layer": peer},
                 device_id_type=MESH,
             ).start()
             return carry
 
-        lax.fori_loop(1, count, send, 0)
-        if c == 3:
-            tex_up = pltpu.make_async_remote_copy(
-                src_ref=stage.at[3, pl.ds(16, 8)],
-                dst_ref=tex_h.at[0],
-                send_sem=tex_send.at[0],
-                recv_sem=tex_recv.at[0],
-                device_id={"tile": up},
-                device_id_type=MESH,
-            )
-            tex_up.start()
-        colb[c, me] = stage[c, :, my_cols]
+        lax.fori_loop(1, count, send_in, 0)
+        colb[g][me] = stage[rows, my_cols]
 
     loads[5].wait()
     loads[6].wait()
@@ -258,20 +277,25 @@
 
     def newton(c):
         group = 4
-
-        def params(g, carry):
-            at = pl.ds(g * group, group)
-            index = colb[c, at, 16:24, :].astype(jnp.int32)
+        g = [c in chunks for chunks in GROUPS].index(True)
+        base = GROUPS[g].index(c) * FIELDS * 8
+
+        def field(f, at):
+            return colb[g][at, base + 8 * f : base + 8 * f + 8, :]
+
+        def params(i, carry):
+            at = pl.ds(i * group, group)
+            index = field(2, at).astype(jnp.int32)
             masks = bits(index, classes)
             values = [lookup(splat, classes, j, index, masks) for j in range(6)]
             for j in range(6):
                 par_c[j, at] = values[j]
-            sat = saturation(colb[c, at, 8:16, :], values[0], values[1], values[2])
+            sat = saturation(field(1, at), values[0], values[1], values[2])
             mold_c[at] = values[4] + values[5] * sat
             return carry
 
         lax.fori_loop(0, count // group, params, 0)
-        hcur[c] = colb[c, :, 0:8, :].reshape(count * 8, LANES)
+        hcur[c] = field(0, slice(None)).reshape(count * 8, LANES)
 
         def step(i, carry):
             h = hcur[c].reshape(shape)
@@ -300,21 +324,6 @@
     def tile_rows(peer):
         return pl.ds(pl.multiple_of(peer * 8, 8), 8)
 
-    def send_halo(c, slot, side, device):
-        def send(k, carry):
-            peer = peer_of(k)
-            pltpu.make_async_remote_copy(
-                src_ref=hcur.at[c, tile_rows(peer)],
-                dst_ref=lay.at[slot, :, my_cols],
-                send_sem=halo_send.at[side],
-                recv_sem=halo_recv.at[side],
-                device_id={"tile": device, "layer": peer},
-                device_id_type=MESH,
-            ).start()
-            return carry
-
-        lax.fori_loop(0, count, send, 0)
-
     def send_back(c):
         def send(k, carry):
             peer = peer_of(k)
@@ -331,55 +340,85 @@
         lax.fori_loop(1, count, send, 0)
         lay[c + 1, :, my_cols] = hcur[c, tile_rows(me), :]
 
-    for c in order:
-        part = colb.at[c, pl.ds(0, count - 1)]
-        pltpu.make_async_copy(part, part, in_recv.at[c]).wait()
-        newton(c)
-        if c == 3:
-            send_halo(3, 0, 0, up)
-        send_back(c)
-
-    tex_up.wait_recv()
-    tex_down = pltpu.make_async_remote_copy(
-        src_ref=stage.at[0, pl.ds(16, 8)],
-        dst_ref=tex_h.at[1],
-        send_sem=tex_send.at[1],
-        recv_sem=tex_recv.at[1],
-        device_id={"tile": down},
-        device_id_type=MESH,
-    )
-    tex_down.start()
-    send_halo(0, 5, 1, down)
-    params_of(lambda cols: tex_h[0, :, cols], 0)
+    def landed(c):
+        part = lay.at[c + 1, :, pl.ds(0, (count - 1) * LANES)]
+        pltpu.make_async_copy(part, part, back_recv.at[c]).wait()
+
+    def forward(c, slot, side):
+        return pltpu.make_async_remote_copy(
+            src_ref=lay.at[c + 1],
+            dst_ref=lay.at[slot],
+            send_sem=halo_send.at[side],
+            recv_sem=halo_recv.at[side],
+            device_id={"tile": up if side == 0 else down},
+            device_id_type=MESH,
+        )
+
+    heads_up, heads_down = forward(3, 0, 0), forward(0, CHUNKS + 1, 1)
+    for g, chunks in enumerate(GROUPS):
+        part = colb[g].at[pl.ds(0, count - 1)]
+        pltpu.make_async_copy(part, part, in_recv.at[g]).wait()
+        for c in chunks:
+            newton(c)
+            send_back(c)
+        if 3 in chunks:
+
+            @pl.when(greets_up)
+            def _():
+                beside(1).wait_recv()
+                beside(0).start()
+
+            landed(3)
+
+            @pl.when(above)
+            def _():
+                heads_up.start()
+
+    @pl.when(first)
+    def _():
+        beside(0).wait_recv()
+        beside(1).start()
+
+    landed(0)
+
+    @pl.when(beneath)
+    def _():
+        heads_down.start()
+
+
+    @pl.when(jnp.logical_not(beneath))
+    def _():
+        tex_h[0] = jnp.zeros(tex_h.shape[1:], F32)
+        lay[0] = lay[1]
+
+    @pl.when(jnp.logical_not(above))
+    def _():
+        tex_h[1] = jnp.zeros(tex_h.shape[1:], F32)
+        lay[CHUNKS + 1] = lay[CHUNKS]
 
     def odd_rows(shape):
         return (lax.broadcasted_iota(jnp.int32, shape, 0) & 1) == 1
 
-    def prepare(src, s):
-        def step(b, carry):
-            cols = pl.ds(pl.multiple_of(b * wide, wide), wide)
-            h = src[s, :, cols]
-            sat = saturation(h, par_l[0, s, :, cols], par_l[1, s, :, cols], par_l[2, s, :, cols])
-            k = par_l[3, s, :, cols] * (sat * sat * sat)
-            odd = odd_rows(h.shape)
-            cond[s, :, cols] = k
-            swap_h[s, :, cols] = jnp.where(odd, pltpu.roll(h, 1, 0), pltpu.roll(h, 7, 0))
-            swap_c[s, :, cols] = jnp.where(odd, pltpu.roll(k, 1, 0), pltpu.roll(k, 7, 0))
-            return carry
-
-        lax.fori_loop(0, blocks, step, 0)
-
-    def advance(src, dst, s):
-        h, k = src[s], cond[s]
+    def prepare(src, dst, s):
+        h = src[s]
+        sat = saturation(h, par_l[0, s], par_l[1, s], par_l[2, s])
+        k = par_l[3, s] * (sat * sat * sat)
+        odd = odd_rows(h.shape)
+        dst[0, s] = k
+        dst[1, s] = jnp.where(odd, pltpu.roll(h, 1, 0), pltpu.roll(h, 7, 0))
+        dst[2, s] = jnp.where(odd, pltpu.roll(k, 1, 0), pltpu.roll(k, 7, 0))
+
+    def advance(src, by, dst, s):
+        h, k = src[s], by[0, s]
         lane = lax.broadcasted_iota(jnp.int32, h.shape, 1)
         flow = (k + pltpu.roll(k, width - 1, 1)) * (pltpu.roll(h, width - 1, 1) - h)
         flow = jnp.where(lane == width - 1, 0.0, flow)
         change = flow - pltpu.roll(flow, 1, 1)
-        change = change + (k + swap_c[s]) * (swap_h[s] - h)
+        change = change + (k + by[2, s]) * (by[1, s] - h)
         odd = odd_rows(h.shape)
         after, before = min(s + 1, CHUNKS + 1), max(s - 1, 0)
-        side_h = jnp.where(odd, swap_h[after], swap_h[before])
-        side_c = jnp.where(odd, swap_c[after], swap_c[before])
+        side_h = jnp.where(odd, by[1, after], by[1, before])
+        side_c = jnp.where(odd, by[2, after], by[2, before])
         side = (k + side_c) * (side_h - h)
         if s == 1:
             side = jnp.where(jnp.logical_and(tile == 0, jnp.logical_not(odd)), 0.0, side)
@@ -387,44 +426,77 @@
             side = jnp.where(jnp.logical_and(tile == tiles - 1, odd), 0.0, side)
         dst[s] = h + (0.5 * OMEGA) * (change + side)
 
-    for c in order:
-        part = lay.at[c + 1, :, pl.ds(0, (count - 1) * LANES)]
-        pltpu.make_async_copy(part, part, back_recv.at[c]).wait()
-        prepare(lay, c + 1)
-    tex_down.wait_recv()
+    prepare(lay, ready, 4)
+    prepare(lay, ready, 1)
+    landed(1)
+    prepare(lay, ready, 2)
+
+    @pl.when(last)
+    def _():
+        beside(1).wait_recv()
+
     params_of(lambda cols: tex_h[1, :, cols], 5)
-    pltpu.make_async_copy(lay.at[5], lay.at[5], halo_recv.at[1]).wait()
-    prepare(lay, 5)
-    for s in (2, 3, 4, 5):
-        advance(lay, lay2, s)
-    pltpu.make_async_copy(lay.at[0], lay.at[0], halo_recv.at[0]).wait()
-    prepare(lay, 0)
-    for s in (0, 1):
-        advance(lay, lay2, s)
-    for s in range(6):
-        prepare(lay2, s)
+
+    def low_side():
+        @pl.when(greeted_below)
+        def _():
+            beside(0).wait_recv()
+
+        params_of(lambda cols: tex_h[0, :, cols], 0)
+
+        @pl.when(beneath)
+        def _():
+            heads_up.wait_recv()
+
+        prepare(lay, ready, 0)
+        for s in (0, 1):
+            advance(lay, ready, lay2, s)
+            prepare(lay2, ready2, s)
+
+    pl.when(jnp.logical_not(first))(low_side)
+
+    @pl.when(above)
+    def _():
+        heads_down.wait_recv()
+
+    prepare(lay, ready, 5)
+    advance(lay, ready, lay2, 5)
+    prepare(lay2, ready2, 5)
+    landed(2)
+    prepare(lay, ready, 3)
+    for s in (2, 3, 4):
+        advance(lay, ready, lay2, s)
+        prepare(lay2, ready2, s)
+    pl.when(first)(low_side)
     for s in (1, 2, 3, 4):
-        advance(lay2, fin, s)
+        advance(lay2, ready2, fin, s)
 
     def unpack(b, carry):
         cols = pl.ds(pl.multiple_of(b * wide, wide), wide)
         for l, rows in enumerate(exchange([fin[c + 1, :, cols] for c in range(CHUNKS)])):
             nat_h[8 * l : 8 * l + 8, cols] = rows
+        pltpu.make_async_copy(nat_h.at[:, cols], out.at[:, cols], load_sem.at[7]).start()
         return carry
 
     lax.fori_loop(0, blocks, unpack, 0)
-    store = pltpu.make_async_copy(nat_h, out, load_sem.at[7])
-    store.start()
+    for g in range(len(GROUPS)):
+        part = colb[g].at[pl.ds(0, count - 1)]
+        pltpu.make_async_copy(part, part, in_send.at[g]).wait()
     for c in range(CHUNKS):
-        part = colb.at[c, pl.ds(0, count - 1)]
-        pltpu.make_async_copy(part, part, in_send.at[c]).wait()
         part = hcur.at[c, pl.ds(0, (count - 1) * 8)]
         pltpu.make_async_copy(part, part, back_send.at[c]).wait()
-    pltpu.make_async_copy(hcur.at[3], hcur.at[3], halo_send.at[0]).wait()
-    pltpu.make_async_copy(hcur.at[0], hcur.at[0], halo_send.at[1]).wait()
-    tex_up.wait_send()
-    tex_down.wait_send()
-    store.wait()
+
+    @pl.when(above)
+    def _():
+        heads_up.wait_send()
+        beside(0).wait_send()
+
+    @pl.when(beneath)
+    def _():
+        heads_down.wait_send()
+        beside(1).wait_send()
+
+    pltpu.make_async_copy(nat_h, out, load_sem.at[7]).wait()
 
 
 def body(pressure, old_pressure, texture, zones, rates, vg_table, approx_inverse):
@@ -449,8 +521,8 @@
             vmem(*flat),
             vmem(*flat),
             vmem(*flat, dtype=jnp.int32),
-            vmem(CHUNKS, FIELDS * 2 * depth, width),
-            vmem(CHUNKS, count, FIELDS * 2 * depth, LANES),
+            vmem(CHUNKS * FIELDS * 2 * depth, width),
+            *(vmem(count, len(g) * FIELDS * 2 * depth, LANES) for g in GROUPS),
             vmem(CHUNKS, count * 2 * depth, LANES),
             vmem(6, *column),
             vmem(*column),
@@ -459,9 +531,8 @@
             vmem(CHUNKS, 8, LANES),
             vmem(*slots),
             vmem(*slots),
-            vmem(*slots),
-            vmem(*slots),
-            vmem(*slots),
+            vmem(3, *slots),
+            vmem(3, *slots),
             vmem(4, *slots),
             vmem(2, 2 * depth, width),
             vmem(*slots),
@@ -472,8 +543,8 @@
             vmem(6, classes, 8, LANES),
             vmem(*approx_inverse.shape),
             pltpu.SemaphoreType.DMA((8,)),
-            pltpu.SemaphoreType.DMA((CHUNKS,)),
-            pltpu.SemaphoreType.DMA((CHUNKS,)),
+            pltpu.SemaphoreType.DMA((len(GROUPS),)),
+            pltpu.SemaphoreType.DMA((len(GROUPS),)),
             pltpu.SemaphoreType.DMA((CHUNKS,)),
             pltpu.SemaphoreType.DMA((CHUNKS,)),
             pltpu.SemaphoreType.DMA((2,)),

time: 44.1 us -> 41.8 us (0.948)
  the two profiles are of different devices: /device:TPU:385 before, /device:TPU:56 now
where the time goes in v3:
time: 41.8 us; the launch traced here: 41.5 us
  Pallas kernels  39.8 us (95%)
  local copies, waits for them, and re-layouts  1.67 us (4%)
    pallas_call x1, Pallas kernels, body(): pl.pallas_call(functools.partial(kernel, count, tiles), out_shape=jax.Sha...  39.8 us
    unnamed x1, local copies, waits for them, and re-layouts  1.67 us

profile of v3, /device:TPU:56, one launch (start us, length us, event | category | flops | bytes accessed | tf_op | source)
XLA Modules:
  0.0 41.5 jit_solution(14449493425266296812)
XLA Ops:
  0.0 39.8 %shard_map.73 = f32[32,2048]{1,0:T(8,128)} custom-call(f32[32,2048]{1,0:T(8,128)} %bitcast.6, f32[32,2048]{1,0:T(8,128)} %bitcast.7, s32[32,2048]{1,0:T(8,128)} %bitcast.8, s32[8,2048]{1,0:T(8,128)} %zones.1, f32[1,16]{1,0:T(1,128)} %bitcast.9, f32[5,12]{1,0:T(8,128)} %table.1, f32[64,64]{1,0:T(8,128)} %inverse.1), custom_call_target="tpu_custom_call" | custom-call | tf_op jit(solution)/shard_map/pallas_call | solution.py:515
  39.8 1.7 %copy.9 = f32[4,8,2048]{2,1,0:T(8,128)} copy(f32[4,8,2048]{2,1,0:T(8,128)} %bitcast.5) | data formatting | bytes 524288

commit v4 on v3

--- a/solution.py
+++ b/solution.py
@@ -14,9 +14,32 @@
 LANES = 128
 CHUNKS = 4
 FIELDS = 3
-GROUPS = ((3, 0), (1, 2))
-ORDER = sum(GROUPS, ())
+HEAD, OLD, TEXTURE = range(FIELDS)
+GROUPS = (
+    tuple((c, f) for c in (3, 0) for f in range(FIELDS)),
+    tuple((c, f) for c in (1, 2) for f in (TEXTURE, OLD)),
+    tuple((c, HEAD) for c in (1, 2)),
+)
+TILES = sum(GROUPS, ())
+SIDE = 4
+TURNS = sorted(
+    range(1, SIDE * SIDE),
+    key=lambda v: (not v & 2, -(v % SIDE) - min(v // SIDE, SIDE - v // SIDE)),
+)
 F32 = jnp.float32
+
+
+def words(values):
+    packed = [sum(v << (4 * i) for i, v in enumerate(values[j : j + 8])) for j in (0, 8)]
+    return [w - (1 << 32) if w >= 1 << 31 else w for w in packed]
+
+
+TURN_WORDS = words(TURNS)
+
+
+def turn(k):
+    word = jnp.where(k < 8, jnp.int32(TURN_WORDS[0]), jnp.int32(TURN_WORDS[1]))
+    return lax.shift_right_logical(word, 4 * lax.rem(k, 8)) & (SIDE * SIDE - 1)
 
 
 def saturation(head, la, n, negp):
@@ -84,6 +107,7 @@
     stage,
     colb_a,
     colb_b,
+    colb_c,
     hcur,
     par_c,
     mold_c,
@@ -96,7 +120,6 @@
     ready2,
     par_l,
     tex_h,
-    fin,
     zone_v,
     rate_v,
     table_v,
@@ -113,7 +136,7 @@
     tex_send,
     tex_recv,
 ):
-    colb = (colb_a, colb_b)
+    colb = (colb_a, colb_b, colb_c)
     me = lax.axis_index("layer")
     tile = lax.axis_index("tile")
     width = press.shape[1]
@@ -126,33 +149,9 @@
     blocks = width // wide
 
     def peer_of(k):
-        return lax.rem(me + k, count)
+        return jnp.bitwise_xor(me, turn(k))
 
     run = tiles // 2
-    above, beneath = tile != tiles - 1, tile != 0
-    last, first = tile == run - 1, tile == run
-    greets_up = jnp.logical_and(above, jnp.logical_not(last))
-    greeted_below = jnp.logical_and(beneath, jnp.logical_not(first))
-
-    def hello(device):
-        pl.semaphore_signal(
-            pltpu.get_barrier_semaphore(), inc=1, device_id=device, device_id_type=MESH
-        )
-
-    def greet(k, carry):
-        hello({"layer": peer_of(k)})
-        return carry
-
-    lax.fori_loop(1, count, greet, 0)
-
-    @pl.when(greets_up)
-    def _():
-        hello({"tile": up})
-
-    @pl.when(first)
-    def _():
-        hello({"tile": down})
-
     my_cols = pl.ds(pl.multiple_of(me * LANES, LANES), LANES)
     loads = [
         pltpu.make_async_copy(table, table_v, load_sem.at[0]),
@@ -165,6 +164,30 @@
     ]
     for load in loads:
         load.start()
+
+    above, beneath = tile != tiles - 1, tile != 0
+    last, first = tile == run - 1, tile == run
+    greets_up = jnp.logical_and(above, jnp.logical_not(last))
+    greeted_below = jnp.logical_and(beneath, jnp.logical_not(first))
+
+    def hello(device):
+        pl.semaphore_signal(
+            pltpu.get_barrier_semaphore(), inc=1, device_id=device, device_id_type=MESH
+        )
+
+    def greet(k, carry):
+        hello({"layer": peer_of(k)})
+        return carry
+
+    lax.fori_loop(0, count - 1, greet, 0)
+
+    @pl.when(greets_up)
+    def _():
+        hello({"tile": up})
+
+    @pl.when(first)
+    def _():
+        hello({"tile": down})
 
     loads[0].wait()
     tab[...] = jnp.ones(tab.shape, F32)
@@ -182,6 +205,9 @@
         for k in range(classes):
             splat[j, k] = jnp.broadcast_to(row[:, k : k + 1], (8, LANES))
 
+    def staged(c, f):
+        return pl.ds(8 * TILES.index((c, f)), 8)
+
     for load in loads[1:4]:
         load.wait()
 
@@ -192,13 +218,10 @@
             if f == 2:
                 rows = [r.astype(F32) for r in rows]
             for c, packed in enumerate(exchange(rows)):
-                stage[pl.ds(ORDER.index(c) * FIELDS * 8 + 8 * f, 8), cols] = packed
+                stage[staged(c, f), cols] = packed
         return carry
 
     lax.fori_loop(0, blocks, pack, 0)
-
-    def at_stage(c):
-        return ORDER.index(c) * FIELDS * 8
 
     def params_of(texture, slot):
         def step(b, carry):
@@ -211,15 +234,12 @@
 
         lax.fori_loop(0, blocks, step, 0)
 
-    for c in range(CHUNKS):
-        params_of(lambda cols, c=c: stage[pl.ds(at_stage(c) + 16, 8), cols], c + 1)
-
     greeted = count - 1 + jnp.where(greeted_below, 1, 0) + jnp.where(last, 1, 0)
     pl.semaphore_wait(pltpu.get_barrier_semaphore(), greeted)
 
     def beside(side):
         return pltpu.make_async_remote_copy(
-            src_ref=stage.at[pl.ds(at_stage(3 if side == 0 else 0) + 16, 8)],
+            src_ref=stage.at[staged(3 if side == 0 else 0, TEXTURE)],
             dst_ref=tex_h.at[side],
             send_sem=tex_send.at[side],
             recv_sem=tex_recv.at[side],
@@ -235,8 +255,10 @@
     def _():
         beside(0).start()
 
-    for g, chunks in enumerate(GROUPS):
-        rows = pl.ds(at_stage(chunks[0]), len(chunks) * FIELDS * 8)
+    start = 0
+    for g, members in enumerate(GROUPS):
+        rows = pl.ds(8 * start, 8 * len(members))
+        start += len(members)
 
         def send_in(k, carry, g=g, rows=rows):
             peer = peer_of(k)
@@ -250,8 +272,11 @@
             ).start()
             return carry
 
-        lax.fori_loop(1, count, send_in, 0)
+        lax.fori_loop(0, count - 1, send_in, 0)
         colb[g][me] = stage[rows, my_cols]
+
+    for c in range(CHUNKS):
+        params_of(lambda cols, c=c: stage[staged(c, TEXTURE), cols], c + 1)
 
     loads[5].wait()
     loads[6].wait()
@@ -275,37 +300,39 @@
         last = pltpu.roll(x[count - 1 :], 2, 1)
         return pltpu.roll(jnp.where(sub3 < 2, jnp.concatenate([x[1:], last], axis=0), x), 6, 1)
 
-    def newton(c):
+    def field(c, f, at):
+        g = [(c, f) in members for members in GROUPS].index(True)
+        row = 8 * GROUPS[g].index((c, f))
+        return colb[g][at, row : row + 8, :]
+
+    def column_params(c):
         group = 4
-        g = [c in chunks for chunks in GROUPS].index(True)
-        base = GROUPS[g].index(c) * FIELDS * 8
-
-        def field(f, at):
-            return colb[g][at, base + 8 * f : base + 8 * f + 8, :]
-
-        def params(i, carry):
+
+        def step(i, carry):
             at = pl.ds(i * group, group)
-            index = field(2, at).astype(jnp.int32)
+            index = field(c, TEXTURE, at).astype(jnp.int32)
             masks = bits(index, classes)
             values = [lookup(splat, classes, j, index, masks) for j in range(6)]
             for j in range(6):
-                par_c[j, at] = values[j]
-            sat = saturation(field(1, at), values[0], values[1], values[2])
-            mold_c[at] = values[4] + values[5] * sat
+                par_c[c, j, at] = values[j]
+            sat = saturation(field(c, OLD, at), values[0], values[1], values[2])
+            mold_c[c, at] = values[4] + values[5] * sat
             return carry
 
-        lax.fori_loop(0, count // group, params, 0)
-        hcur[c] = field(0, slice(None)).reshape(count * 8, LANES)
+        lax.fori_loop(0, count // group, step, 0)
+
+    def newton(c):
+        hcur[c] = field(c, HEAD, slice(None)).reshape(count * 8, LANES)
 
         def step(i, carry):
             h = hcur[c].reshape(shape)
-            sat = saturation(h, par_c[0], par_c[1], par_c[2])
-            k = par_c[3] * (sat * sat * sat)
+            sat = saturation(h, par_c[c, 0], par_c[c, 1], par_c[c, 2])
+            k = par_c[c, 3] * (sat * sat * sat)
             flux = (0.5 * (k + below(k))) * (h - below(h) + 1.0)
             shifted = jnp.concatenate([ghost[c][None], flux[:-1]], axis=0)
             above = pltpu.roll(jnp.where(sub3 >= 6, shifted, flux), 2, 1)
-            moisture = par_c[4] + par_c[5] * sat
-            misfit = (moisture - mold_c[...]) + (flux - above)
+            moisture = par_c[c, 4] + par_c[c, 5] * sat
+            misfit = (moisture - mold_c[c]) + (flux - above)
             mis_c[...] = misfit.reshape(count * 8, LANES)
             x = jnp.concatenate(
                 [mis_c[pl.ds(y, layers, stride=2), :] for y in range(2)], axis=1
@@ -337,7 +364,7 @@
             ).start()
             return carry
 
-        lax.fori_loop(1, count, send, 0)
+        lax.fori_loop(0, count - 1, send, 0)
         lay[c + 1, :, my_cols] = hcur[c, tile_rows(me), :]
 
     def landed(c):
@@ -355,24 +382,30 @@
         )
 
     heads_up, heads_down = forward(3, 0, 0), forward(0, CHUNKS + 1, 1)
-    for g, chunks in enumerate(GROUPS):
+    def arrived(g):
         part = colb[g].at[pl.ds(0, count - 1)]
         pltpu.make_async_copy(part, part, in_recv.at[g]).wait()
-        for c in chunks:
-            newton(c)
-            send_back(c)
-        if 3 in chunks:
-
-            @pl.when(greets_up)
-            def _():
-                beside(1).wait_recv()
-                beside(0).start()
-
-            landed(3)
-
-            @pl.when(above)
-            def _():
-                heads_up.start()
+
+    arrived(0)
+    for c in (3, 0):
+        column_params(c)
+        newton(c)
+        send_back(c)
+
+    @pl.when(greets_up)
+    def _():
+        beside(1).wait_recv()
+        beside(0).start()
+
+    landed(3)
+
+    @pl.when(above)
+    def _():
+        heads_up.start()
+
+    arrived(1)
+    for c in (1, 2):
+        column_params(c)
 
     @pl.when(first)
     def _():
@@ -385,6 +418,10 @@
     def _():
         heads_down.start()
 
+    arrived(2)
+    for c in (1, 2):
+        newton(c)
+        send_back(c)
 
     @pl.when(jnp.logical_not(beneath))
     def _():
@@ -404,27 +441,31 @@
         sat = saturation(h, par_l[0, s], par_l[1, s], par_l[2, s])
         k = par_l[3, s] * (sat * sat * sat)
         odd = odd_rows(h.shape)
+        other_h = jnp.where(odd, pltpu.roll(h, 1, 0), pltpu.roll(h, 7, 0))
+        other_k = jnp.where(odd, pltpu.roll(k, 1, 0), pltpu.roll(k, 7, 0))
         dst[0, s] = k
-        dst[1, s] = jnp.where(odd, pltpu.roll(h, 1, 0), pltpu.roll(h, 7, 0))
-        dst[2, s] = jnp.where(odd, pltpu.roll(k, 1, 0), pltpu.roll(k, 7, 0))
-
-    def advance(src, by, dst, s):
-        h, k = src[s], by[0, s]
+        dst[1, s] = other_h
+        dst[2, s] = other_k
         lane = lax.broadcasted_iota(jnp.int32, h.shape, 1)
         flow = (k + pltpu.roll(k, width - 1, 1)) * (pltpu.roll(h, width - 1, 1) - h)
         flow = jnp.where(lane == width - 1, 0.0, flow)
-        change = flow - pltpu.roll(flow, 1, 1)
-        change = change + (k + by[2, s]) * (by[1, s] - h)
+        dst[3, s] = flow - pltpu.roll(flow, 1, 1) + (k + other_k) * (other_h - h)
+
+    def advanced(src, by, s, cols):
+        h, k = src[s, :, cols], by[0, s, :, cols]
         odd = odd_rows(h.shape)
         after, before = min(s + 1, CHUNKS + 1), max(s - 1, 0)
-        side_h = jnp.where(odd, by[1, after], by[1, before])
-        side_c = jnp.where(odd, by[2, after], by[2, before])
-        side = (k + side_c) * (side_h - h)
+        side_h = jnp.where(odd, by[1, after, :, cols], by[1, before, :, cols])
+        side_k = jnp.where(odd, by[2, after, :, cols], by[2, before, :, cols])
+        side = (k + side_k) * (side_h - h)
         if s == 1:
             side = jnp.where(jnp.logical_and(tile == 0, jnp.logical_not(odd)), 0.0, side)
         if s == CHUNKS:
             side = jnp.where(jnp.logical_and(tile == tiles - 1, odd), 0.0, side)
-        dst[s] = h + (0.5 * OMEGA) * (change + side)
+        return h + (0.5 * OMEGA) * (by[3, s, :, cols] + side)
+
+    def advance(src, by, dst, s):
+        dst[s] = advanced(src, by, s, slice(None))
 
     prepare(lay, ready, 4)
     prepare(lay, ready, 1)
@@ -468,17 +509,15 @@
         advance(lay, ready, lay2, s)
         prepare(lay2, ready2, s)
     pl.when(first)(low_side)
-    for s in (1, 2, 3, 4):
-        advance(lay2, ready2, fin, s)
-
-    def unpack(b, carry):
+    def finish(b, carry):
         cols = pl.ds(pl.multiple_of(b * wide, wide), wide)
-        for l, rows in enumerate(exchange([fin[c + 1, :, cols] for c in range(CHUNKS)])):
+        tops = [advanced(lay2, ready2, c + 1, cols) for c in range(CHUNKS)]
+        for l, rows in enumerate(exchange(tops)):
             nat_h[8 * l : 8 * l + 8, cols] = rows
         pltpu.make_async_copy(nat_h.at[:, cols], out.at[:, cols], load_sem.at[7]).start()
         return carry
 
-    lax.fori_loop(0, blocks, unpack, 0)
+    lax.fori_loop(0, blocks, finish, 0)
     for g in range(len(GROUPS)):
         part = colb[g].at[pl.ds(0, count - 1)]
         pltpu.make_async_copy(part, part, in_send.at[g]).wait()
@@ -522,20 +561,19 @@
             vmem(*flat),
             vmem(*flat, dtype=jnp.int32),
             vmem(CHUNKS * FIELDS * 2 * depth, width),
-            *(vmem(count, len(g) * FIELDS * 2 * depth, LANES) for g in GROUPS),
+            *(vmem(count, len(g) * 2 * depth, LANES) for g in GROUPS),
             vmem(CHUNKS, count * 2 * depth, LANES),
-            vmem(6, *column),
-            vmem(*column),
+            vmem(CHUNKS, 6, *column),
+            vmem(CHUNKS, *column),
             vmem(count * 2 * depth, LANES),
             vmem(count * 2 * depth, LANES),
             vmem(CHUNKS, 8, LANES),
             vmem(*slots),
             vmem(*slots),
-            vmem(3, *slots),
-            vmem(3, *slots),
+            vmem(4, *slots),
+            vmem(4, *slots),
             vmem(4, *slots),
             vmem(2, 2 * depth, width),
-            vmem(*slots),
             vmem(tall, LANES, dtype=jnp.int32),
             vmem(1, rates.shape[0]),
             vmem(*vg_table.shape),

time: 41.8 us -> 41 us (0.981)
  Pallas kernels: 39.8 us -> 39.2 us
    pallas_call x1, Pallas kernels: 39.8 us -> 39.2 us  [body(): pl.pallas_call(functools.partial(kernel, count, tiles), out_shape=jax.Sha...]
where the time goes in v4:
time: 41 us; the launch traced here: 40.9 us
  Pallas kernels  39.2 us (96%)
  local copies, waits for them, and re-layouts  1.67 us (4%)
    pallas_call x1, Pallas kernels, body(): pl.pallas_call(functools.partial(kernel, count, tiles), out_shape=jax.Sha...  39.2 us
    unnamed x1, local copies, waits for them, and re-layouts  1.67 us

profile of v4, /device:TPU:56, one launch (start us, length us, event | category | flops | bytes accessed | tf_op | source)
XLA Modules:
  0.0 40.9 jit_solution(15595888905792229388)
XLA Ops:
  0.0 39.2 %shard_map.73 = f32[32,2048]{1,0:T(8,128)} custom-call(f32[32,2048]{1,0:T(8,128)} %bitcast.6, f32[32,2048]{1,0:T(8,128)} %bitcast.7, s32[32,2048]{1,0:T(8,128)} %bitcast.8, s32[8,2048]{1,0:T(8,128)} %zones.1, f32[1,16]{1,0:T(1,128)} %bitcast.9, f32[5,12]{1,0:T(8,128)} %table.1, f32[64,64]{1,0:T(8,128)} %inverse.1), custom_call_target="tpu_custom_call" | custom-call | tf_op jit(solution)/shard_map/pallas_call | solution.py:554
  39.2 1.7 %copy.9 = f32[4,8,2048]{2,1,0:T(8,128)} copy(f32[4,8,2048]{2,1,0:T(8,128)} %bitcast.5) | data formatting | bytes 524288

commit v5 on v4

--- a/solution.py
+++ b/solution.py
@@ -17,10 +17,11 @@
 HEAD, OLD, TEXTURE = range(FIELDS)
 GROUPS = (
     tuple((c, f) for c in (3, 0) for f in range(FIELDS)),
-    tuple((c, f) for c in (1, 2) for f in (TEXTURE, OLD)),
-    tuple((c, HEAD) for c in (1, 2)),
+    tuple((c, f) for c in (1, 2) for f in range(FIELDS)),
 )
 TILES = sum(GROUPS, ())
+PAIRS = ((3, 0), (1, 2))
+PLACES = (0, 4, 1, 2, 3, 5)
 SIDE = 4
 TURNS = sorted(
     range(1, SIDE * SIDE),
@@ -34,7 +35,7 @@
     return [w - (1 << 32) if w >= 1 << 31 else w for w in packed]
 
 
-TURN_WORDS = words(TURNS)
+TURN_WORDS = words(TURNS + [0])
 
 
 def turn(k):
@@ -107,7 +108,6 @@
     stage,
     colb_a,
     colb_b,
-    colb_c,
     hcur,
     par_c,
     mold_c,
@@ -136,7 +136,7 @@
     tex_send,
     tex_recv,
 ):
-    colb = (colb_a, colb_b, colb_c)
+    colb = (colb_a, colb_b)
     me = lax.axis_index("layer")
     tile = lax.axis_index("tile")
     width = press.shape[1]
@@ -185,9 +185,14 @@
     def _():
         hello({"tile": up})
 
+    def greet_below(k, carry):
+        hello({"tile": down, "layer": peer_of(k)})
+        return carry
+
     @pl.when(first)
     def _():
-        hello({"tile": down})
+        lax.fori_loop(0, count, greet_below, 0)
+
 
     loads[0].wait()
     tab[...] = jnp.ones(tab.shape, F32)
@@ -234,7 +239,7 @@
 
         lax.fori_loop(0, blocks, step, 0)
 
-    greeted = count - 1 + jnp.where(greeted_below, 1, 0) + jnp.where(last, 1, 0)
+    greeted = count - 1 + jnp.where(greeted_below, 1, 0) + jnp.where(last, count, 0)
     pl.semaphore_wait(pltpu.get_barrier_semaphore(), greeted)
 
     def beside(side):
@@ -321,60 +326,67 @@
 
         lax.fori_loop(0, count // group, step, 0)
 
-    def newton(c):
-        hcur[c] = field(c, HEAD, slice(None)).reshape(count * 8, LANES)
-
-        def step(i, carry):
-            h = hcur[c].reshape(shape)
-            sat = saturation(h, par_c[c, 0], par_c[c, 1], par_c[c, 2])
-            k = par_c[c, 3] * (sat * sat * sat)
-            flux = (0.5 * (k + below(k))) * (h - below(h) + 1.0)
-            shifted = jnp.concatenate([ghost[c][None], flux[:-1]], axis=0)
-            above = pltpu.roll(jnp.where(sub3 >= 6, shifted, flux), 2, 1)
-            moisture = par_c[c, 4] + par_c[c, 5] * sat
-            misfit = (moisture - mold_c[c]) + (flux - above)
-            mis_c[...] = misfit.reshape(count * 8, LANES)
-            x = jnp.concatenate(
-                [mis_c[pl.ds(y, layers, stride=2), :] for y in range(2)], axis=1
-            )
+    def newton(p):
+        chunks = PAIRS[p]
+        for i, c in enumerate(chunks):
+            hcur[p, :, 8 * i : 8 * i + 8, :] = field(c, HEAD, slice(None))
+
+        def step(_, carry):
+            for i, c in enumerate(chunks):
+                h = hcur[p, :, 8 * i : 8 * i + 8, :]
+                sat = saturation(h, par_c[c, 0], par_c[c, 1], par_c[c, 2])
+                k = par_c[c, 3] * (sat * sat * sat)
+                flux = (0.5 * (k + below(k))) * (h - below(h) + 1.0)
+                shifted = jnp.concatenate([ghost[c][None], flux[:-1]], axis=0)
+                above_it = pltpu.roll(jnp.where(sub3 >= 6, shifted, flux), 2, 1)
+                moisture = par_c[c, 4] + par_c[c, 5] * sat
+                misfit = (moisture - mold_c[c]) + (flux - above_it)
+                mis_c[i] = misfit.reshape(count * 8, LANES)
+            parts = [(i, y) for i in range(len(chunks)) for y in range(2)]
+            x = jnp.concatenate([mis_c[i, pl.ds(y, layers, stride=2), :] for i, y in parts], axis=1)
             hi = x.astype(jnp.bfloat16)
             lo = (x - hi.astype(F32)).astype(jnp.bfloat16)
             stacked = jnp.concatenate([hi, hi, lo], axis=0)
             update = jnp.dot(inv_all, stacked, preferred_element_type=F32)
-            for y in range(2):
-                upd_c[pl.ds(y, layers, stride=2), :] = update[:, y * LANES : (y + 1) * LANES]
-            hcur[c] = hcur[c] - upd_c[...]
+            for j, (i, y) in enumerate(parts):
+                upd_c[i, pl.ds(y, layers, stride=2), :] = update[:, j * LANES : (j + 1) * LANES]
+            for i in range(len(chunks)):
+                rows = slice(8 * i, 8 * i + 8)
+                hcur[p, :, rows, :] = hcur[p, :, rows, :] - upd_c[i].reshape(shape)
             return carry
 
         lax.fori_loop(0, ITERS, step, 0)
 
-    def tile_rows(peer):
-        return pl.ds(pl.multiple_of(peer * 8, 8), 8)
-
-    def send_back(c):
+    def slot_rows(s):
+        return pl.ds(8 * PLACES.index(s), 8)
+
+    def pair_rows(p):
+        return pl.ds(8 * PLACES.index(PAIRS[p][0] + 1), 16)
+
+    def send_back(p):
         def send(k, carry):
             peer = peer_of(k)
             pltpu.make_async_remote_copy(
-                src_ref=hcur.at[c, tile_rows(peer)],
-                dst_ref=lay.at[c + 1, :, my_cols],
-                send_sem=back_send.at[c],
-                recv_sem=back_recv.at[c],
+                src_ref=hcur.at[p, peer],
+                dst_ref=lay.at[pair_rows(p), my_cols],
+                send_sem=back_send.at[p],
+                recv_sem=back_recv.at[p],
                 device_id={"layer": peer},
                 device_id_type=MESH,
             ).start()
             return carry
 
         lax.fori_loop(0, count - 1, send, 0)
-        lay[c + 1, :, my_cols] = hcur[c, tile_rows(me), :]
-
-    def landed(c):
-        part = lay.at[c + 1, :, pl.ds(0, (count - 1) * LANES)]
-        pltpu.make_async_copy(part, part, back_recv.at[c]).wait()
+        lay[pair_rows(p), my_cols] = hcur[p, me]
+
+    def landed(p):
+        part = lay.at[pair_rows(p), pl.ds(0, (count - 1) * LANES)]
+        pltpu.make_async_copy(part, part, back_recv.at[p]).wait()
 
     def forward(c, slot, side):
         return pltpu.make_async_remote_copy(
-            src_ref=lay.at[c + 1],
-            dst_ref=lay.at[slot],
+            src_ref=lay.at[slot_rows(c + 1)],
+            dst_ref=lay.at[slot_rows(slot)],
             send_sem=halo_send.at[side],
             recv_sem=halo_recv.at[side],
             device_id={"tile": up if side == 0 else down},
@@ -387,57 +399,73 @@
         pltpu.make_async_copy(part, part, in_recv.at[g]).wait()
 
     arrived(0)
-    for c in (3, 0):
+    for c in PAIRS[0]:
         column_params(c)
-        newton(c)
-        send_back(c)
+    newton(0)
+
+    def send_up(k, carry):
+        peer = peer_of(k)
+        pltpu.make_async_remote_copy(
+            src_ref=hcur.at[0, peer, pl.ds(0, 8)],
+            dst_ref=lay.at[slot_rows(0), my_cols],
+            send_sem=halo_send.at[0],
+            recv_sem=halo_recv.at[0],
+            device_id={"tile": up, "layer": peer},
+            device_id_type=MESH,
+        ).start()
+        return carry
+
+    @pl.when(last)
+    def _():
+        lax.fori_loop(0, count, send_up, 0)
+
+    send_back(0)
 
     @pl.when(greets_up)
     def _():
         beside(1).wait_recv()
         beside(0).start()
 
-    landed(3)
-
-    @pl.when(above)
+    landed(0)
+
+    @pl.when(greets_up)
     def _():
         heads_up.start()
 
-    arrived(1)
-    for c in (1, 2):
-        column_params(c)
 
     @pl.when(first)
     def _():
         beside(0).wait_recv()
         beside(1).start()
 
-    landed(0)
-
     @pl.when(beneath)
     def _():
         heads_down.start()
 
-    arrived(2)
-    for c in (1, 2):
-        newton(c)
-        send_back(c)
+    arrived(1)
+    for c in PAIRS[1]:
+        column_params(c)
+    newton(1)
+    send_back(1)
 
     @pl.when(jnp.logical_not(beneath))
     def _():
         tex_h[0] = jnp.zeros(tex_h.shape[1:], F32)
-        lay[0] = lay[1]
+        lay[slot_rows(0)] = lay[slot_rows(1)]
 
     @pl.when(jnp.logical_not(above))
     def _():
         tex_h[1] = jnp.zeros(tex_h.shape[1:], F32)
-        lay[CHUNKS + 1] = lay[CHUNKS]
+        lay[slot_rows(CHUNKS + 1)] = lay[slot_rows(CHUNKS)]
 
     def odd_rows(shape):
         return (lax.broadcasted_iota(jnp.int32, shape, 0) & 1) == 1
 
+    def head(src, s, cols):
+        return src[slot_rows(s), cols] if src is lay else src[s, :, cols]
+
     def prepare(src, dst, s):
-        h = src[s]
+        h = head(src, s, slice(None))
         sat = saturation(h, par_l[0, s], par_l[1, s], par_l[2, s])
         k = par_l[3, s] * (sat * sat * sat)
         odd = odd_rows(h.shape)
@@ -452,7 +480,7 @@
         dst[3, s] = flow - pltpu.roll(flow, 1, 1) + (k + other_k) * (other_h - h)
 
     def advanced(src, by, s, cols):
-        h, k = src[s, :, cols], by[0, s, :, cols]
+        h, k = head(src, s, cols), by[0, s, :, cols]
         odd = odd_rows(h.shape)
         after, before = min(s + 1, CHUNKS + 1), max(s - 1, 0)
         side_h = jnp.where(odd, by[1, after, :, cols], by[1, before, :, cols])
@@ -469,8 +497,6 @@
 
     prepare(lay, ready, 4)
     prepare(lay, ready, 1)
-    landed(1)
-    prepare(lay, ready, 2)
 
     @pl.when(last)
     def _():
@@ -490,9 +516,8 @@
             heads_up.wait_recv()
 
         prepare(lay, ready, 0)
-        for s in (0, 1):
-            advance(lay, ready, lay2, s)
-            prepare(lay2, ready2, s)
+        advance(lay, ready, lay2, 0)
+        prepare(lay2, ready2, 0)
 
     pl.when(jnp.logical_not(first))(low_side)
 
@@ -503,12 +528,15 @@
     prepare(lay, ready, 5)
     advance(lay, ready, lay2, 5)
     prepare(lay2, ready2, 5)
-    landed(2)
+    landed(1)
+    prepare(lay, ready, 2)
     prepare(lay, ready, 3)
     for s in (2, 3, 4):
         advance(lay, ready, lay2, s)
         prepare(lay2, ready2, s)
     pl.when(first)(low_side)
+    advance(lay, ready, lay2, 1)
+    prepare(lay2, ready2, 1)
     def finish(b, carry):
         cols = pl.ds(pl.multiple_of(b * wide, wide), wide)
         tops = [advanced(lay2, ready2, c + 1, cols) for c in range(CHUNKS)]
@@ -521,9 +549,9 @@
     for g in range(len(GROUPS)):
         part = colb[g].at[pl.ds(0, count - 1)]
         pltpu.make_async_copy(part, part, in_send.at[g]).wait()
-    for c in range(CHUNKS):
-        part = hcur.at[c, pl.ds(0, (count - 1) * 8)]
-        pltpu.make_async_copy(part, part, back_send.at[c]).wait()
+    for p in range(len(PAIRS)):
+        part = hcur.at[p, pl.ds(0, count - 1)]
+        pltpu.make_async_copy(part, part, back_send.at[p]).wait()
 
     @pl.when(above)
     def _():
@@ -562,13 +590,13 @@
             vmem(*flat, dtype=jnp.int32),
             vmem(CHUNKS * FIELDS * 2 * depth, width),
             *(vmem(count, len(g) * 2 * depth, LANES) for g in GROUPS),
-            vmem(CHUNKS, count * 2 * depth, LANES),
+            vmem(len(PAIRS), count, 4 * depth, LANES),
             vmem(CHUNKS, 6, *column),
             vmem(CHUNKS, *column),
-            vmem(count * 2 * depth, LANES),
-            vmem(count * 2 * depth, LANES),
+            vmem(2, count * 2 * depth, LANES),
+            vmem(2, count * 2 * depth, LANES),
             vmem(CHUNKS, 8, LANES),
-            vmem(*slots),
+            vmem((CHUNKS + 2) * 2 * depth, width),
             vmem(*slots),
             vmem(4, *slots),
             vmem(4, *slots),
@@ -583,8 +611,8 @@
             pltpu.SemaphoreType.DMA((8,)),
             pltpu.SemaphoreType.DMA((len(GROUPS),)),
             pltpu.SemaphoreType.DMA((len(GROUPS),)),
-            pltpu.SemaphoreType.DMA((CHUNKS,)),
-            pltpu.SemaphoreType.DMA((CHUNKS,)),
+            pltpu.SemaphoreType.DMA((len(PAIRS),)),
+            pltpu.SemaphoreType.DMA((len(PAIRS),)),
             pltpu.SemaphoreType.DMA((2,)),
             pltpu.SemaphoreType.DMA((2,)),
             pltpu.SemaphoreType.DMA((2,)),

time: 41 us -> 40.1 us (0.978)
  Pallas kernels: 39.2 us -> 38.1 us
    pallas_call x1, Pallas kernels: 39.2 us -> 38.1 us  [body(): pl.pallas_call(functools.partial(kernel, count, tiles), out_shape=jax.Sha...]
where the time goes in v5:
time: 40.1 us; the launch traced here: 39.8 us
  Pallas kernels  38.1 us (95%)
  local copies, waits for them, and re-layouts  1.67 us (4%)
    pallas_call x1, Pallas kernels, body(): pl.pallas_call(functools.partial(kernel, count, tiles), out_shape=jax.Sha...  38.1 us
    unnamed x1, local copies, waits for them, and re-layouts  1.67 us

profile of v5, /device:TPU:56, one launch (start us, length us, event | category | flops | bytes accessed | tf_op | source)
XLA Modules:
  0.0 39.8 jit_solution(14599461825553316869)
XLA Ops:
  0.0 38.1 %shard_map.73 = f32[32,2048]{1,0:T(8,128)} custom-call(f32[32,2048]{1,0:T(8,128)} %bitcast.6, f32[32,2048]{1,0:T(8,128)} %bitcast.7, s32[32,2048]{1,0:T(8,128)} %bitcast.8, s32[8,2048]{1,0:T(8,128)} %zones.1, f32[1,16]{1,0:T(1,128)} %bitcast.9, f32[5,12]{1,0:T(8,128)} %table.1, f32[64,64]{1,0:T(8,128)} %inverse.1), custom_call_target="tpu_custom_call" | custom-call | tf_op jit(solution)/shard_map/pallas_call | solution.py:582
  38.1 1.7 %copy.9 = f32[4,8,2048]{2,1,0:T(8,128)} copy(f32[4,8,2048]{2,1,0:T(8,128)} %bitcast.5) | data formatting | bytes 524288

commit v6 on v5

--- a/solution.py
+++ b/solution.py
@@ -15,11 +15,15 @@
 CHUNKS = 4
 FIELDS = 3
 HEAD, OLD, TEXTURE = range(FIELDS)
-GROUPS = (
-    tuple((c, f) for c in (3, 0) for f in range(FIELDS)),
-    tuple((c, f) for c in (1, 2) for f in range(FIELDS)),
+SEGMENTS = (
+    tuple((c, f) for c in (1, 2) for f in (TEXTURE, OLD)),
+    tuple((c, f) for c in (3, 0) for f in (TEXTURE, OLD)),
+    tuple((c, HEAD) for c in (3, 0)),
+    tuple((c, HEAD) for c in (1, 2)),
 )
-TILES = sum(GROUPS, ())
+TILES = sum(SEGMENTS, ())
+USUAL = ((0, 1), (2, 3))
+BORDER = ((1, 2), (0,), (3,))
 PAIRS = ((3, 0), (1, 2))
 PLACES = (0, 4, 1, 2, 3, 5)
 SIDE = 4
@@ -106,8 +110,7 @@
     nat_o,
     nat_t,
     stage,
-    colb_a,
-    colb_b,
+    colb,
     hcur,
     par_c,
     mold_c,
@@ -136,7 +139,6 @@
     tex_send,
     tex_recv,
 ):
-    colb = (colb_a, colb_b)
     me = lax.axis_index("layer")
     tile = lax.axis_index("tile")
     width = press.shape[1]
@@ -169,6 +171,9 @@
     last, first = tile == run - 1, tile == run
     greets_up = jnp.logical_and(above, jnp.logical_not(last))
     greeted_below = jnp.logical_and(beneath, jnp.logical_not(first))
+    odd_tile = lax.rem(tile, 2) == 1
+    straight_down = jnp.logical_and(greeted_below, jnp.logical_not(odd_tile))
+    last_chip = lax.rem(tile, run) >= run - 2
 
     def hello(device):
         pl.semaphore_signal(
@@ -181,7 +186,15 @@
 
     lax.fori_loop(0, count - 1, greet, 0)
 
-    @pl.when(greets_up)
+    def greet_above(k, carry):
+        hello({"tile": up, "layer": peer_of(k)})
+        return carry
+
+    @pl.when(jnp.logical_and(greets_up, odd_tile))
+    def _():
+        lax.fori_loop(0, count, greet_above, 0)
+
+    @pl.when(jnp.logical_and(greets_up, jnp.logical_not(odd_tile)))
     def _():
         hello({"tile": up})
 
@@ -239,7 +252,8 @@
 
         lax.fori_loop(0, blocks, step, 0)
 
-    greeted = count - 1 + jnp.where(greeted_below, 1, 0) + jnp.where(last, count, 0)
+    greeted = count - 1 + jnp.where(last, count, 0)
+    greeted = greeted + jnp.where(straight_down, count, jnp.where(greeted_below, 1, 0))
     pl.semaphore_wait(pltpu.get_barrier_semaphore(), greeted)
 
     def beside(side):
@@ -260,25 +274,38 @@
     def _():
         beside(0).start()
 
-    start = 0
-    for g, members in enumerate(GROUPS):
-        rows = pl.ds(8 * start, 8 * len(members))
-        start += len(members)
-
-        def send_in(k, carry, g=g, rows=rows):
-            peer = peer_of(k)
-            pltpu.make_async_remote_copy(
-                src_ref=stage.at[rows, pl.ds(pl.multiple_of(peer * LANES, LANES), LANES)],
-                dst_ref=colb[g].at[me],
-                send_sem=in_send.at[g],
-                recv_sem=in_recv.at[g],
-                device_id={"layer": peer},
-                device_id_type=MESH,
-            ).start()
-            return carry
-
-        lax.fori_loop(0, count - 1, send_in, 0)
-        colb[g][me] = stage[rows, my_cols]
+    def rows_of(segments):
+        start = 8 * sum(len(members) for members in SEGMENTS[: segments[0]])
+        return pl.ds(start, 8 * sum(len(SEGMENTS[g]) for g in segments))
+
+    def send_copies(copies):
+        for g, segments in enumerate(copies):
+            rows = rows_of(segments)
+
+            def send_in(k, carry, g=g, rows=rows):
+                peer = peer_of(k)
+                pltpu.make_async_remote_copy(
+                    src_ref=stage.at[rows, pl.ds(pl.multiple_of(peer * LANES, LANES), LANES)],
+                    dst_ref=colb.at[me, rows],
+                    send_sem=in_send.at[g],
+                    recv_sem=in_recv.at[g],
+                    device_id={"layer": peer},
+                    device_id_type=MESH,
+                ).start()
+                return carry
+
+            lax.fori_loop(0, count - 1, send_in, 0)
+
+    def others(copies, g, sems):
+        part = colb.at[pl.ds(0, count - 1), rows_of(copies[g])]
+        pltpu.make_async_copy(part, part, sems.at[g]).wait()
+
+    def in_border(usual, border):
+        pl.when(jnp.logical_not(last))(usual)
+        pl.when(last)(border)
+
+    in_border(lambda: send_copies(USUAL), lambda: send_copies(BORDER))
+    colb[me] = stage[:, my_cols]
 
     for c in range(CHUNKS):
         params_of(lambda cols, c=c: stage[staged(c, TEXTURE), cols], c + 1)
@@ -306,9 +333,8 @@
         return pltpu.roll(jnp.where(sub3 < 2, jnp.concatenate([x[1:], last], axis=0), x), 6, 1)
 
     def field(c, f, at):
-        g = [(c, f) in members for members in GROUPS].index(True)
-        row = 8 * GROUPS[g].index((c, f))
-        return colb[g][at, row : row + 8, :]
+        row = 8 * TILES.index((c, f))
+        return colb[at, row : row + 8, :]
 
     def column_params(c):
         group = 4
@@ -394,32 +420,57 @@
         )
 
     heads_up, heads_down = forward(3, 0, 0), forward(0, CHUNKS + 1, 1)
-    def arrived(g):
-        part = colb[g].at[pl.ds(0, count - 1)]
-        pltpu.make_async_copy(part, part, in_recv.at[g]).wait()
-
-    arrived(0)
+    in_border(lambda: others(USUAL, 0, in_recv), lambda: others(BORDER, 0, in_recv))
     for c in PAIRS[0]:
         column_params(c)
+
+    @pl.when(jnp.logical_not(last))
+    def _():
+        for c in PAIRS[1]:
+            column_params(c)
+
+    pl.when(jnp.logical_not(last))(lambda: others(USUAL, 1, in_recv))
     newton(0)
 
-    def send_up(k, carry):
-        peer = peer_of(k)
-        pltpu.make_async_remote_copy(
-            src_ref=hcur.at[0, peer, pl.ds(0, 8)],
-            dst_ref=lay.at[slot_rows(0), my_cols],
-            send_sem=halo_send.at[0],
-            recv_sem=halo_recv.at[0],
-            device_id={"tile": up, "layer": peer},
-            device_id_type=MESH,
-        ).start()
-        return carry
+    def send_straight(row, slot, side, device):
+        def send(k, carry):
+            peer = peer_of(k)
+            pltpu.make_async_remote_copy(
+                src_ref=hcur.at[0, peer, pl.ds(row, 8)],
+                dst_ref=lay.at[slot_rows(slot), my_cols],
+                send_sem=halo_send.at[side],
+                recv_sem=halo_recv.at[side],
+                device_id={"tile": device, "layer": peer},
+                device_id_type=MESH,
+            ).start()
+            return carry
+
+        lax.fori_loop(0, count, send, 0)
 
     @pl.when(last)
     def _():
-        lax.fori_loop(0, count, send_up, 0)
-
-    send_back(0)
+        send_straight(0, 0, 0, up)
+
+    @pl.when(jnp.logical_and(straight_down, jnp.logical_not(last_chip)))
+    def _():
+        send_straight(8, CHUNKS + 1, 1, down)
+
+    pl.when(jnp.logical_not(last))(lambda: send_back(0))
+
+    @pl.when(jnp.logical_and(straight_down, last_chip))
+    def _():
+        send_straight(8, CHUNKS + 1, 1, down)
+
+    @pl.when(last)
+    def _():
+        others(BORDER, 1, in_recv)
+        for c in PAIRS[1]:
+            column_params(c)
+        others(BORDER, 2, in_recv)
+        send_back(0)
+
+    newton(1)
+    send_back(1)
 
     @pl.when(greets_up)
     def _():
@@ -438,15 +489,9 @@
         beside(0).wait_recv()
         beside(1).start()
 
-    @pl.when(beneath)
+    @pl.when(jnp.logical_and(beneath, jnp.logical_not(straight_down)))
     def _():
         heads_down.start()
-
-    arrived(1)
-    for c in PAIRS[1]:
-        column_params(c)
-    newton(1)
-    send_back(1)
 
     @pl.when(jnp.logical_not(beneath))
     def _():
@@ -546,9 +591,11 @@
         return carry
 
     lax.fori_loop(0, blocks, finish, 0)
-    for g in range(len(GROUPS)):
-        part = colb[g].at[pl.ds(0, count - 1)]
-        pltpu.make_async_copy(part, part, in_send.at[g]).wait()
+    def sent(copies):
+        for g in range(len(copies)):
+            others(copies, g, in_send)
+
+    in_border(lambda: sent(USUAL), lambda: sent(BORDER))
     for p in range(len(PAIRS)):
         part = hcur.at[p, pl.ds(0, count - 1)]
         pltpu.make_async_copy(part, part, back_send.at[p]).wait()
@@ -589,7 +636,7 @@
             vmem(*flat),
             vmem(*flat, dtype=jnp.int32),
             vmem(CHUNKS * FIELDS * 2 * depth, width),
-            *(vmem(count, len(g) * 2 * depth, LANES) for g in GROUPS),
+            vmem(count, len(TILES) * 2 * depth, LANES),
             vmem(len(PAIRS), count, 4 * depth, LANES),
             vmem(CHUNKS, 6, *column),
             vmem(CHUNKS, *column),
@@ -609,8 +656,8 @@
             vmem(6, classes, 8, LANES),
             vmem(*approx_inverse.shape),
             pltpu.SemaphoreType.DMA((8,)),
-            pltpu.SemaphoreType.DMA((len(GROUPS),)),
-            pltpu.SemaphoreType.DMA((len(GROUPS),)),
+            pltpu.SemaphoreType.DMA((len(BORDER),)),
+            pltpu.SemaphoreType.DMA((len(BORDER),)),
             pltpu.SemaphoreType.DMA((len(PAIRS),)),
             pltpu.SemaphoreType.DMA((len(PAIRS),)),
             pltpu.SemaphoreType.DMA((2,)),

time: 40.1 us -> 39.1 us (0.975)
  the two profiles are of different devices: /device:TPU:56 before, /device:TPU:193 now
where the time goes in v6:
time: 39.1 us; the launch traced here: 38.9 us
  Pallas kernels  37.2 us (95%)
  local copies, waits for them, and re-layouts  1.67 us (4%)
    pallas_call x1, Pallas kernels, body(): pl.pallas_call(functools.partial(kernel, count, tiles), out_shape=jax.Sha...  37.2 us
    unnamed x1, local copies, waits for them, and re-layouts  1.67 us

profile of v6, /device:TPU:193, one launch (start us, length us, event | category | flops | bytes accessed | tf_op | source)
XLA Modules:
  0.0 38.9 jit_solution(14659378894957614973)
XLA Ops:
  0.0 37.2 %shard_map.73 = f32[32,2048]{1,0:T(8,128)} custom-call(f32[32,2048]{1,0:T(8,128)} %bitcast.6, f32[32,2048]{1,0:T(8,128)} %bitcast.7, s32[32,2048]{1,0:T(8,128)} %bitcast.8, s32[8,2048]{1,0:T(8,128)} %zones.1, f32[1,16]{1,0:T(1,128)} %bitcast.9, f32[5,12]{1,0:T(8,128)} %table.1, f32[64,64]{1,0:T(8,128)} %inverse.1), custom_call_target="tpu_custom_call" | custom-call | tf_op jit(solution)/shard_map/pallas_call | solution.py:629
  37.2 1.7 %copy.9 = f32[4,8,2048]{2,1,0:T(8,128)} copy(f32[4,8,2048]{2,1,0:T(8,128)} %bitcast.5) | data formatting | bytes 524288

commit v7 on v6

--- a/solution.py
+++ b/solution.py
@@ -22,7 +22,7 @@
     tuple((c, HEAD) for c in (1, 2)),
 )
 TILES = sum(SEGMENTS, ())
-USUAL = ((0, 1), (2, 3))
+USUAL = ((0, 1), (2,), (3,))
 BORDER = ((1, 2), (0,), (3,))
 PAIRS = ((3, 0), (1, 2))
 PLACES = (0, 4, 1, 2, 3, 5)
@@ -173,7 +173,6 @@
     greeted_below = jnp.logical_and(beneath, jnp.logical_not(first))
     odd_tile = lax.rem(tile, 2) == 1
     straight_down = jnp.logical_and(greeted_below, jnp.logical_not(odd_tile))
-    last_chip = lax.rem(tile, run) >= run - 2
 
     def hello(device):
         pl.semaphore_signal(
@@ -451,24 +450,21 @@
     def _():
         send_straight(0, 0, 0, up)
 
-    @pl.when(jnp.logical_and(straight_down, jnp.logical_not(last_chip)))
+    @pl.when(straight_down)
     def _():
         send_straight(8, CHUNKS + 1, 1, down)
 
     pl.when(jnp.logical_not(last))(lambda: send_back(0))
-
-    @pl.when(jnp.logical_and(straight_down, last_chip))
-    def _():
-        send_straight(8, CHUNKS + 1, 1, down)
 
     @pl.when(last)
     def _():
         others(BORDER, 1, in_recv)
         for c in PAIRS[1]:
             column_params(c)
+        send_back(0)
         others(BORDER, 2, in_recv)
-        send_back(0)
-
+
+    pl.when(jnp.logical_not(last))(lambda: others(USUAL, 2, in_recv))
     newton(1)
     send_back(1)
 
@@ -519,6 +515,8 @@
         dst[0, s] = k
         dst[1, s] = other_h
         dst[2, s] = other_k
+        if src is lay2 and s in (0, CHUNKS + 1):
+            return
         lane = lax.broadcasted_iota(jnp.int32, h.shape, 1)
         flow = (k + pltpu.roll(k, width - 1, 1)) * (pltpu.roll(h, width - 1, 1) - h)
         flow = jnp.where(lane == width - 1, 0.0, flow)
@@ -549,39 +547,36 @@
 
     params_of(lambda cols: tex_h[1, :, cols], 5)
 
-    def low_side():
-        @pl.when(greeted_below)
-        def _():
-            beside(0).wait_recv()
-
-        params_of(lambda cols: tex_h[0, :, cols], 0)
-
-        @pl.when(beneath)
-        def _():
-            heads_up.wait_recv()
-
-        prepare(lay, ready, 0)
-        advance(lay, ready, lay2, 0)
-        prepare(lay2, ready2, 0)
-
-    pl.when(jnp.logical_not(first))(low_side)
-
-    @pl.when(above)
-    def _():
-        heads_down.wait_recv()
-
-    prepare(lay, ready, 5)
-    advance(lay, ready, lay2, 5)
-    prepare(lay2, ready2, 5)
+    @pl.when(greeted_below)
+    def _():
+        beside(0).wait_recv()
+
+    params_of(lambda cols: tex_h[0, :, cols], 0)
     landed(1)
     prepare(lay, ready, 2)
     prepare(lay, ready, 3)
-    for s in (2, 3, 4):
+    for s in (2, 3):
         advance(lay, ready, lay2, s)
         prepare(lay2, ready2, s)
-    pl.when(first)(low_side)
-    advance(lay, ready, lay2, 1)
-    prepare(lay2, ready2, 1)
+
+    @pl.when(above)
+    def _():
+        heads_down.wait_recv()
+
+    prepare(lay, ready, 5)
+    for s in (4, 5):
+        advance(lay, ready, lay2, s)
+        prepare(lay2, ready2, s)
+
+    @pl.when(beneath)
+    def _():
+        heads_up.wait_recv()
+
+    prepare(lay, ready, 0)
+    for s in (0, 1):
+        advance(lay, ready, lay2, s)
+        prepare(lay2, ready2, s)
+
     def finish(b, carry):
         cols = pl.ds(pl.multiple_of(b * wide, wide), wide)
         tops = [advanced(lay2, ready2, c + 1, cols) for c in range(CHUNKS)]

time: 39.1 us -> 38.7 us (0.990)
  the two profiles are of different devices: /device:TPU:193 before, /device:TPU:448 now
where the time goes in v7:
time: 38.7 us; the launch traced here: 38.6 us
  Pallas kernels  36.9 us (95%)
  local copies, waits for them, and re-layouts  1.67 us (4%)
    pallas_call x1, Pallas kernels, body(): pl.pallas_call(functools.partial(kernel, count, tiles), out_shape=jax.Sha...  36.9 us
    unnamed x1, local copies, waits for them, and re-layouts  1.67 us

profile of v7, /device:TPU:448, one launch (start us, length us, event | category | flops | bytes accessed | tf_op | source)
XLA Modules:
  0.0 38.6 jit_solution(1950281097724046240)
XLA Ops:
  0.0 36.9 %shard_map.73 = f32[32,2048]{1,0:T(8,128)} custom-call(f32[32,2048]{1,0:T(8,128)} %bitcast.6, f32[32,2048]{1,0:T(8,128)} %bitcast.7, s32[32,2048]{1,0:T(8,128)} %bitcast.8, s32[8,2048]{1,0:T(8,128)} %zones.1, f32[1,16]{1,0:T(1,128)} %bitcast.9, f32[5,12]{1,0:T(8,128)} %table.1, f32[64,64]{1,0:T(8,128)} %inverse.1), custom_call_target="tpu_custom_call" | custom-call | tf_op jit(solution)/shard_map/pallas_call | solution.py:624
  36.9 1.7 %copy.9 = f32[4,8,2048]{2,1,0:T(8,128)} copy(f32[4,8,2048]{2,1,0:T(8,128)} %bitcast.5) | data formatting | bytes 524288

commit v8 on v7

--- a/solution.py
+++ b/solution.py
@@ -22,8 +22,7 @@
     tuple((c, HEAD) for c in (1, 2)),
 )
 TILES = sum(SEGMENTS, ())
-USUAL = ((0, 1), (2,), (3,))
-BORDER = ((1, 2), (0,), (3,))
+COPIES = ((1, 2), (0,), (3,))
 PAIRS = ((3, 0), (1, 2))
 PLACES = (0, 4, 1, 2, 3, 5)
 SIDE = 4
@@ -277,33 +276,27 @@
         start = 8 * sum(len(members) for members in SEGMENTS[: segments[0]])
         return pl.ds(start, 8 * sum(len(SEGMENTS[g]) for g in segments))
 
-    def send_copies(copies):
-        for g, segments in enumerate(copies):
-            rows = rows_of(segments)
-
-            def send_in(k, carry, g=g, rows=rows):
-                peer = peer_of(k)
-                pltpu.make_async_remote_copy(
-                    src_ref=stage.at[rows, pl.ds(pl.multiple_of(peer * LANES, LANES), LANES)],
-                    dst_ref=colb.at[me, rows],
-                    send_sem=in_send.at[g],
-                    recv_sem=in_recv.at[g],
-                    device_id={"layer": peer},
-                    device_id_type=MESH,
-                ).start()
-                return carry
-
-            lax.fori_loop(0, count - 1, send_in, 0)
-
-    def others(copies, g, sems):
-        part = colb.at[pl.ds(0, count - 1), rows_of(copies[g])]
+    for g, segments in enumerate(COPIES):
+        rows = rows_of(segments)
+
+        def send_in(k, carry, g=g, rows=rows):
+            peer = peer_of(k)
+            pltpu.make_async_remote_copy(
+                src_ref=stage.at[rows, pl.ds(pl.multiple_of(peer * LANES, LANES), LANES)],
+                dst_ref=colb.at[me, rows],
+                send_sem=in_send.at[g],
+                recv_sem=in_recv.at[g],
+                device_id={"layer": peer},
+                device_id_type=MESH,
+            ).start()
+            return carry
+
+        lax.fori_loop(0, count - 1, send_in, 0)
+
+    def others(g, sems):
+        part = colb.at[pl.ds(0, count - 1), rows_of(COPIES[g])]
         pltpu.make_async_copy(part, part, sems.at[g]).wait()
 
-    def in_border(usual, border):
-        pl.when(jnp.logical_not(last))(usual)
-        pl.when(last)(border)
-
-    in_border(lambda: send_copies(USUAL), lambda: send_copies(BORDER))
     colb[me] = stage[:, my_cols]
 
     for c in range(CHUNKS):
@@ -419,16 +412,10 @@
         )
 
     heads_up, heads_down = forward(3, 0, 0), forward(0, CHUNKS + 1, 1)
-    in_border(lambda: others(USUAL, 0, in_recv), lambda: others(BORDER, 0, in_recv))
+    others(0, in_recv)
     for c in PAIRS[0]:
         column_params(c)
 
-    @pl.when(jnp.logical_not(last))
-    def _():
-        for c in PAIRS[1]:
-            column_params(c)
-
-    pl.when(jnp.logical_not(last))(lambda: others(USUAL, 1, in_recv))
     newton(0)
 
     def send_straight(row, slot, side, device):
@@ -454,17 +441,13 @@
     def _():
         send_straight(8, CHUNKS + 1, 1, down)
 
-    pl.when(jnp.logical_not(last))(lambda: send_back(0))
-
-    @pl.when(last)
-    def _():
-        others(BORDER, 1, in_recv)
-        for c in PAIRS[1]:
-            column_params(c)
-        send_back(0)
-        others(BORDER, 2, in_recv)
-
-    pl.when(jnp.logical_not(last))(lambda: others(USUAL, 2, in_recv))
+
+    others(1, in_recv)
+    for c in PAIRS[1]:
+        column_params(c)
+    send_back(0)
+    others(2, in_recv)
+
     newton(1)
     send_back(1)
 
@@ -586,11 +569,8 @@
         return carry
 
     lax.fori_loop(0, blocks, finish, 0)
-    def sent(copies):
-        for g in range(len(copies)):
-            others(copies, g, in_send)
-
-    in_border(lambda: sent(USUAL), lambda: sent(BORDER))
+    for g in range(len(COPIES)):
+        others(g, in_send)
     for p in range(len(PAIRS)):
         part = hcur.at[p, pl.ds(0, count - 1)]
         pltpu.make_async_copy(part, part, back_send.at[p]).wait()
@@ -651,8 +631,8 @@
             vmem(6, classes, 8, LANES),
             vmem(*approx_inverse.shape),
             pltpu.SemaphoreType.DMA((8,)),
-            pltpu.SemaphoreType.DMA((len(BORDER),)),
-            pltpu.SemaphoreType.DMA((len(BORDER),)),
+            pltpu.SemaphoreType.DMA((len(COPIES),)),
+            pltpu.SemaphoreType.DMA((len(COPIES),)),
             pltpu.SemaphoreType.DMA((len(PAIRS),)),
             pltpu.SemaphoreType.DMA((len(PAIRS),)),
             pltpu.SemaphoreType.DMA((2,)),

time: 38.7 us -> 37.5 us (0.969)
  the two profiles are of different devices: /device:TPU:448 before, /device:TPU:56 now
where the time goes in v8:
time: 37.5 us; the launch traced here: 37.1 us
  Pallas kernels  35.4 us (94%)
  local copies, waits for them, and re-layouts  1.67 us (4%)
    pallas_call x1, Pallas kernels, body(): pl.pallas_call(functools.partial(kernel, count, tiles), out_shape=jax.Sha...  35.4 us
    unnamed x1, local copies, waits for them, and re-layouts  1.67 us

profile of v8, /device:TPU:56, one launch (start us, length us, event | category | flops | bytes accessed | tf_op | source)
XLA Modules:
  0.0 37.1 jit_solution(987292381268035030)
XLA Ops:
  0.0 35.4 %shard_map.73 = f32[32,2048]{1,0:T(8,128)} custom-call(f32[32,2048]{1,0:T(8,128)} %bitcast.6, f32[32,2048]{1,0:T(8,128)} %bitcast.7, s32[32,2048]{1,0:T(8,128)} %bitcast.8, s32[8,2048]{1,0:T(8,128)} %zones.1, f32[1,16]{1,0:T(1,128)} %bitcast.9, f32[5,12]{1,0:T(8,128)} %table.1, f32[64,64]{1,0:T(8,128)} %inverse.1), custom_call_target="tpu_custom_call" | custom-call | tf_op jit(solution)/shard_map/pallas_call | solution.py:604
  35.4 1.7 %copy.9 = f32[4,8,2048]{2,1,0:T(8,128)} copy(f32[4,8,2048]{2,1,0:T(8,128)} %bitcast.5) | data formatting | bytes 524288

commit v9 on v8

--- a/solution.py
+++ b/solution.py
@@ -146,7 +146,7 @@
     layers = count * depth
     down = lax.rem(tile + tiles - 1, tiles)
     up = lax.rem(tile + 1, tiles)
-    wide = 512
+    wide = 1024
     blocks = width // wide
 
     def peer_of(k):

time: 37.5 us -> 37.5 us (level)
  no operation moved by 1% of the time
where the time goes in v9:
time: 37.5 us; the launch traced here: 37.1 us
  Pallas kernels  35.4 us (94%)
  local copies, waits for them, and re-layouts  1.67 us (4%)
    pallas_call x1, Pallas kernels, body(): pl.pallas_call(functools.partial(kernel, count, tiles), out_shape=jax.Sha...  35.4 us
    unnamed x1, local copies, waits for them, and re-layouts  1.67 us

profile of v9, /device:TPU:56, one launch (start us, length us, event | category | flops | bytes accessed | tf_op | source)
XLA Modules:
  0.0 37.1 jit_solution(9310657333144423677)
XLA Ops:
  0.0 35.4 %shard_map.73 = f32[32,2048]{1,0:T(8,128)} custom-call(f32[32,2048]{1,0:T(8,128)} %bitcast.6, f32[32,2048]{1,0:T(8,128)} %bitcast.7, s32[32,2048]{1,0:T(8,128)} %bitcast.8, s32[8,2048]{1,0:T(8,128)} %zones.1, f32[1,16]{1,0:T(1,128)} %bitcast.9, f32[5,12]{1,0:T(8,128)} %table.1, f32[64,64]{1,0:T(8,128)} %inverse.1), custom_call_target="tpu_custom_call" | custom-call | tf_op jit(solution)/shard_map/pallas_call | solution.py:604
  35.4 1.7 %copy.9 = f32[4,8,2048]{2,1,0:T(8,128)} copy(f32[4,8,2048]{2,1,0:T(8,128)} %bitcast.5) | data formatting | bytes 524288
